TPU v7x, 256 devices: a whole 4x4x8 slice. The times are simulated.
256 devices in a mesh: gx: 32 (over z, x), yz: 8 (over y, core).
Axes of the slice: x: 4, y: 4, z: 8, core: 2. Of those that a mesh axis runs over, the one named last changes fastest.
Arguments:
- state: float32 [3, 256, 256, 256], P(None, 'gx', 'yz'), may hold values from -5 to 5
- direction: float32 [3, 256, 256, 256], P(None, 'gx', 'yz'), may hold values from -16 to 16
- xxt_rows: float32 [8192, 8192], P(('gx', 'yz')), may hold values from -0.0625 to 0.0625
- coarse_ids: int32 [256, 128], P(('gx', 'yz')), may hold values from 0 to 31, as said below
Outputs:
- next_basis: float32 [3, 256, 256, 256], P(None, 'gx', 'yz')
- hessenberg: float32 [2], replicated
Inputs may be any that keep to these rules, and one draw needn't show every extreme that they name: `coarse_ids`: each row names its partition's 32 coarse unknowns, each exactly 128 // 32 times.
All inputs are finite; a program needn't handle non-finite values.
Results may differ from a plain program's by a relative error of at most 0.0003.
Values sent between devices are 32-bit elements; how exact they have to be, the bound alone decides.
A program may use at most 128 MiB of HBM per device.

v0:
```python
import jax
import jax.numpy as jnp
import numpy as np
from jax import lax
from jax.sharding import PartitionSpec as P

viscosity = 0.05
epsilon = 1e-06


def padded_2(value, sides, width):
    for axis, dim in sides:
        peers, length = (lax.axis_size(axis), value.shape[dim])
        up = [(i, (i + 1) % peers) for i in range(peers - 1)]
        down = [(j, i) for i, j in up]
        last = lax.slice_in_dim(value, length - width, length, axis=dim)
        first = lax.slice_in_dim(value, 0, width, axis=dim)
        before = lax.ppermute(last, axis, up)
        after = lax.ppermute(first, axis, down)
        value = jnp.concatenate([before, value, after], axis=dim)
    return value


def tables():
    points = np.array(
        [
            -1.0,
            -0.8717401485096066,
            -0.5917001814331423,
            -0.2092992179024789,
            0.2092992179024789,
            0.5917001814331423,
            0.8717401485096066,
            1.0,
        ]
    )
    weights = np.array(
        [
            1.0 / 28.0,
            0.2107042271435061,
            0.3411226924835044,
            0.4124587946587038,
            0.4124587946587038,
            0.3411226924835044,
            0.2107042271435061,
            1.0 / 28.0,
        ]
    )
    differ = points[:, None] - points[None, :]
    positions = np.arange(8)
    differ[positions, positions] = 1.0
    barycentric = 1.0 / np.prod(differ, axis=1)
    derivative = barycentric[None, :] / barycentric[:, None] / differ
    derivative[positions, positions] = 0.0
    derivative[positions, positions] = -derivative.sum(axis=1)
    return (jnp.asarray(derivative, jnp.float32), jnp.asarray(weights, jnp.float32))


def apply_along(tensor, matrix, spatial):
    full_shape = tensor.shape
    blocks = tensor.reshape(
        full_shape[:spatial] + (full_shape[spatial] // 8, 8) + full_shape[spatial + 1 :]
    )
    result = jnp.tensordot(
        blocks, matrix, axes=((spatial + 1,), (1,)), precision=lax.Precision.HIGHEST
    )
    result = jnp.moveaxis(result, -1, spatial + 1)
    return result.reshape(full_shape)


def per_point(vectors):
    return vectors[0][:, None, None] * vectors[1][None, :, None] * vectors[2][None, None, :]


def mass_field(full_shape, point_w):
    return per_point([jnp.tile(point_w, full_shape[spatial] // 8) for spatial in (1, 2, 3)])


def multiplicity(full_shape):
    vectors = []
    for spatial in (1, 2, 3):
        position = jnp.arange(full_shape[spatial]) % 8
        vectors.append(jnp.where((position == 0) | (position == 7), 0.5, 1.0).astype(jnp.float32))
    return per_point(vectors)


def walls_of(full_shape, starts, totals):
    vectors = []
    for spatial in (1, 2, 3):
        global_pos = starts[spatial - 1] + jnp.arange(full_shape[spatial])
        vectors.append(
            ((global_pos > 0) & (global_pos < totals[spatial - 1] - 1)).astype(jnp.float32)
        )
    return per_point(vectors)


def fold_dim(tensor, spatial, padded):
    extent = tensor.shape[spatial]
    following = lax.slice_in_dim(padded, 2, extent + 2, axis=spatial)
    before = lax.slice_in_dim(padded, 0, extent, axis=spatial)
    position = lax.broadcasted_iota(jnp.int32, tensor.shape, spatial) % 8
    return tensor + jnp.where(position == 7, following, 0.0) + jnp.where(position == 0, before, 0.0)


def zero_pad(tensor, spatial):
    widths = [(0, 0)] * tensor.ndim
    widths[spatial] = (1, 1)
    return jnp.pad(tensor, widths)


def element_apply(state, state_grads, vector, mass_w, derivative):
    vector_grads = [apply_along(vector, derivative, spatial) for spatial in (1, 2, 3)]
    convect = jnp.zeros_like(vector)
    for spatial in (1, 2, 3):
        convect = (
            convect
            + state[spatial - 1][None] * vector_grads[spatial - 1]
            + vector[spatial - 1][None] * state_grads[spatial - 1]
        )
    result = mass_w * convect
    for spatial in (1, 2, 3):
        result = result + viscosity * apply_along(
            mass_w * vector_grads[spatial - 1], derivative.T, spatial
        )
    return result


def element_sums(tensor):
    comps, size_a, size_b, size_c = tensor.shape
    return tensor.reshape(comps, size_a // 8, 8, size_b // 8, 8, size_c // 8, 8).sum(axis=(2, 4, 6))


def spread(values):
    return jnp.repeat(jnp.repeat(jnp.repeat(values, 8, axis=1), 8, axis=2), 8, axis=3)


def shards(state, direction, xxt_rows, coarse_ids):
    derivative, point_w = tables()
    full_shape = state.shape
    slabs = lax.axis_size("gx")
    columns = lax.axis_size("yz")
    starts = (lax.axis_index("gx") * full_shape[1], lax.axis_index("yz") * full_shape[2], 0)
    totals = (full_shape[1] * slabs, full_shape[2] * columns, full_shape[3])
    mass_w = mass_field(full_shape, point_w)
    wall_mask = walls_of(full_shape, starts, totals)
    state_grads = [apply_along(state, derivative, spatial) for spatial in (1, 2, 3)]

    def assemble(local_out):
        padded = padded_2(local_out, (("gx", 1),), 1)
        merged = fold_dim(local_out, 1, padded)
        padded = padded_2(merged, (("yz", 2),), 1)
        merged = fold_dim(merged, 2, padded)
        merged = fold_dim(merged, 3, zero_pad(merged, 3))
        return merged * wall_mask

    first_image = assemble(element_apply(state, state_grads, direction, mass_w, derivative))
    elem_totals = element_sums(first_image * mass_w)
    elem_count = coarse_ids.shape[1]
    coarse_count = xxt_rows.shape[0]
    onehot = (
        coarse_ids[0][:, None] == lax.broadcasted_iota(jnp.int32, (elem_count, coarse_count), 1)
    ).astype(jnp.float32)
    coarse_b = jnp.dot(elem_totals.reshape(3, elem_count), onehot, precision=lax.Precision.HIGHEST)
    partial_y = jnp.dot(coarse_b, xxt_rows, precision=lax.Precision.HIGHEST)
    coarse_y = lax.psum(partial_y, ("gx", "yz"))
    coarse_c = jnp.dot(coarse_y, xxt_rows.T, precision=lax.Precision.HIGHEST)
    correction = jnp.dot(coarse_c, onehot.T, precision=lax.Precision.HIGHEST).reshape(
        elem_totals.shape
    )
    coarse_field = spread(correction)
    probe_field = first_image + coarse_field
    second = assemble(element_apply(state, state_grads, probe_field, mass_w, derivative))
    weight = multiplicity(full_shape)
    weight_total = 343.0 * elem_count * slabs * columns
    proj_sum, probe_sum = lax.psum(
        (jnp.sum(weight * second * probe_field), jnp.sum(weight * probe_field * probe_field)),
        ("gx", "yz"),
    )
    projection_coef = proj_sum / weight_total / (probe_sum / weight_total + epsilon)
    remainder = second - projection_coef * probe_field
    rest_mean = lax.psum(jnp.sum(weight * remainder * remainder), ("gx", "yz")) / weight_total
    rms_scale = jnp.sqrt(rest_mean + epsilon)
    return (remainder / rms_scale, jnp.stack([projection_coef, rms_scale]))


def solution(mesh):
    return jax.shard_map(
        shards,
        mesh=mesh,
        in_specs=(
            P(None, "gx", "yz", None),
            P(None, "gx", "yz", None),
            P(("gx", "yz"), None),
            P(("gx", "yz"), None),
        ),
        out_specs=(P(None, "gx", "yz", None), P()),
        check_vma=False,
    )
```

profile of v0, /device:TPU:1, one launch (start us, length us, event | category | flops | bytes accessed | tf_op | source)
XLA Modules:
  0.0 589.2 jit_solution(1562435540378775972)
XLA Ops:
  11.8 3.1 copy.130
  16.8 2.2 copy.135
  25.6 3.7 copy.131
  29.3 6.3 %convolution_bitcast_fusion.1 = f32[3,8,32,32,8]{3,4,2,1,0:T(8,128)} fusion(f32[8,8,1,1,1]{1,0,4,3,2:T(8,128)S(1)} %copy-done.23, f32[3,8,32,32,8]{3,4,2,1,0:T(8,128)} %copy.131), kind=kOutput, calls=%fused_computation.7 | convolution fusion | flops 18874368 | bytes 1573120 | tf_op jit(solution)/shard_map/dot_general | solution.py:64
  35.5 3.8 copy.132
  39.3 6.5 %fusion.4 = f32[3,8,32,32,8]{3,4,2,1,0:T(8,128)} fusion(f32[8,8,1,1,1]{1,0,4,3,2:T(8,128)S(1)} %copy-done.23, f32[3,8,32,32,8]{3,4,2,1,0:T(8,128)} %convolution_bitcast_fusion.1, f32[8,32,32,8]{2,3,1,0:T(8,128)S(1)} %copy-done.4), kind=kOutput, calls=%fused_computation.4 | convolution fusion | flops 19267584 | bytes 1835264 | tf_op jit(solution)/shard_map/dot_general | solution.py:64
  45.8 3.8 copy.143
  49.6 3.1 copy.144
  60.3 3.1 copy.133
  63.4 3.7 copy.136
  67.1 6.2 %convolution_bitcast_fusion = f32[3,8,32,32,8]{3,4,2,1,0:T(8,128)} fusion(f32[8,8,1,1,1]{1,0,4,3,2:T(8,128)S(1)} %copy-done.23, f32[3,8,32,32,8]{3,4,2,1,0:T(8,128)} %copy.136), kind=kOutput, calls=%fused_computation.6 | convolution fusion | flops 18874368 | bytes 1573120 | tf_op jit(solution)/shard_map/dot_general | solution.py:64
  73.3 3.7 copy.137
  76.9 2.5 copy.138
  81.3 4.3 fusion.18
  87.9 4.6 collective-permute-start.1
  96.2 5.7 collective-permute-start.2
  111.1 246.9 %all-reduce.5.cloned.1.call-done = f32[3,8192]{1,0:T(4,128)} async-done(((f32[3,8192]{1,0:T(4,128)}), f32[3,8192]{1,0:T(4,128)}) %all-reduce.5.cloned.1.call-update) | async-done | bytes 98320 | tf_op jit(solution)/shard_map/psum | solution.py:165
  360.5 2.5 copy.149
  363.0 3.7 copy.150
  366.7 5.0 fusion.90
  373.4 4.6 fusion.7
  378.0 3.7 copy.151
  382.7 2.7 fusion.12
  389.3 3.7 copy.158
  393.0 3.1 copy.159
  396.1 3.4 copy.152
  401.1 4.4 fusion.21
  407.0 4.0 collective-permute-start.5
  413.0 5.0 collective-permute-start.6
  418.0 2.9 collective-permute-start.7
  423.3 79.4 %all-reduce.2 = (f32[]{:T(128)}, f32[]{:T(128)}) all-reduce(f32[]{:T(128)} %get-tuple-element.11, f32[]{:T(128)} %get-tuple-element.10), channel_id=1, replica_groups=mesh['gx'=32,'yz'=8] {'gx','yz'}, use_global_device_ids=true, to_apply=%region_4.5 | all-reduce | flops 2 | bytes 16 | tf_op jit(solution)/shard_map/psum | solution.py:175
  504.8 74.6 %psum.31 = f32[]{:T(128)} all-reduce(f32[]{:T(128)} %fusion.49), channel_id=1, replica_groups=mesh['gx'=32,'yz'=8] {'gx','yz'}, use_global_device_ids=true, to_apply=%region_8.9 | all-reduce | flops 1 | bytes 8 | tf_op jit(solution)/shard_map/psum | solution.py:181
  (155 shorter events, 56.4 us)
Async XLA Ops:
  7.2 102.5 %copy-start = (f32[32,8192]{1,0:T(8,128)S(1)}, f32[32,8192]{1,0:T(8,128)}, u32[]{:S(2)}) copy-start(f32[32,8192]{1,0:T(8,128)} %param.8) | copy-start | bytes 3145732
  7.2 7.7 %copy-start.3 = (f32[3,8,32,256]{3,2,1,0:T(8,128)S(1)}, f32[3,8,32,256]{3,2,1,0:T(8,128)}, u32[]{:S(2)}) copy-start(f32[3,8,32,256]{3,2,1,0:T(8,128)} %param.7) | copy-start | bytes 2359300
  7.2 350.8 %all-reduce.5.cloned.1.call-start = ((), (), s32[]{:S(2)}) async-start(), calls=%async_computation | async-start | bytes 262144 | tf_op jit(solution)/shard_map/psum | solution.py:165
  8.9 6.9 %copy-start.2 = (f32[3,8,32,256]{3,2,1,0:T(8,128)S(1)}, f32[3,8,32,256]{3,2,1,0:T(8,128)}, u32[]{:S(2)}) copy-start(f32[3,8,32,256]{3,2,1,0:T(8,128)} %param.6) | copy-start | bytes 2359300
  16.8 4.7 copy-start.24
  19.0 6.5 %copy-start.25 = (f32[8]{0:T(128)S(1)}, f32[8]{0:T(128)}, u32[]{:S(2)}) copy-start(f32[8]{0:T(128)} %constant.109.clone) | copy-start | bytes 100
  52.8 52.4 %copy-start.10 = (f32[8,32,256]{2,0,1:T(8,128)}, f32[8,32,256]{2,0,1:T(8,128)S(1)}, u32[]{:S(2)}) copy-start(f32[8,32,256]{2,0,1:T(8,128)S(1)} %broadcast_multiply_fusion.4) | copy-start | bytes 786436
  52.9 4.8 copy-start.19
  54.3 5.1 copy-start.17
  56.6 24.7 %copy-start.12 = (f32[8,32,256]{2,0,1:T(8,128)}, f32[8,32,256]{2,0,1:T(8,128)S(1)}, u32[]{:S(2)}) copy-start(f32[8,32,256]{2,0,1:T(8,128)S(1)} %copy.121) | copy-start | bytes 786436
  56.8 24.5 %copy-start.13 = (f32[8,32,256]{2,0,1:T(8,128)}, f32[8,32,256]{2,0,1:T(8,128)S(1)}, u32[]{:S(2)}) copy-start(f32[8,32,256]{2,0,1:T(8,128)S(1)} %copy.125) | copy-start | bytes 786436
  79.4 6.3 %copy-start.9 = (f32[3,8,32,256]{3,1,2,0:T(8,128)}, f32[3,8,32,256]{3,1,2,0:T(8,128)S(1)}, u32[]{:S(2)}) copy-start(f32[3,8,32,256]{3,1,2,0:T(8,128)S(1)} %copy.138) | copy-start | bytes 2359300
  81.3 4.4 copy-start.7
  86.6 6.2 %collective-permute-start = (f32[3,1,32,256]{3,1,2,0:T(1,128)}, f32[3,1,32,256]{3,1,2,0:T(1,128)S(1)}, u32[]{:S(2)}, u32[]{:S(2)}) collective-permute-start(f32[3,1,32,256]{3,1,2,0:T(1,128)} %get-tuple-element.26), channel_id=1, source_target_pairs={{8,0},{16,8},{24,16},{32,24},{40,32},{48,40},{56,48},{64,56},{72,6... | collective-permute-start | bytes 294920 | tf_op jit(solution)/shard_map/ppermute | solution.py:19
  87.9 6.2 %collective-permute-start.1 = (f32[3,1,32,256]{3,1,2,0:T(1,128)S(1)}, f32[3,1,32,256]{3,1,2,0:T(1,128)S(1)}, u32[]{:S(2)}, u32[]{:S(2)}) collective-permute-start(f32[3,1,32,256]{3,1,2,0:T(1,128)S(1)} %get-tuple-element.27), channel_id=1, source_target_pairs={{0,8},{8,16},{16,24},{24,32},{32,40},{40,48},{48,56},{56,64},{64,7... | collective-permute-start | bytes 294920 | tf_op jit(solution)/shard_map/ppermute | solution.py:18
  92.5 15.3 %copy-start.26 = (s32[8]{0:T(128)}, s32[8]{0:T(128)S(1)}, u32[]{:S(2)}) copy-start(s32[8]{0:T(128)S(1)} %get-tuple-element.35) | copy-start | bytes 100
  92.5 15.3 %copy-start.28 = (pred[8]{0:T(512)(128)(4,1)}, pred[8]{0:T(512)(128)(4,1)S(1)}, u32[]{:S(2)}) copy-start(pred[8]{0:T(512)(128)(4,1)S(1)} %compare_and_fusion.2) | copy-start | bytes 28
  92.6 15.2 %copy-start.30 = (pred[256]{0:T(512)(128)(4,1)}, pred[256]{0:T(512)(128)(4,1)S(1)}, u32[]{:S(2)}) copy-start(pred[256]{0:T(512)(128)(4,1)S(1)} %compare_and_fusion) | copy-start | bytes 772
  92.8 15.0 %copy-start.15 = (f32[8,32,256]{2,0,1:T(8,128)}, f32[8,32,256]{2,0,1:T(8,128)S(1)}, u32[]{:S(2)}) copy-start(f32[8,32,256]{2,0,1:T(8,128)S(1)} %broadcast_multiply_fusion.2) | copy-start | bytes 786436
  96.2 7.7 %collective-permute-start.2 = (f32[3,8,1,256]{3,1,2,0:T(8,128)S(1)}, f32[3,8,1,256]{3,1,2,0:T(8,128)S(1)}, u32[]{:S(2)}, u32[]{:S(2)}) collective-permute-start(f32[3,8,1,256]{3,1,2,0:T(8,128)S(1)} %get-tuple-element.24), channel_id=1, source_target_pairs={{1,0},{2,1},{3,2},{4,3},{5,4},{6,5},{7,6},{9,8},{10,9},{11,10},{12... | collective-permute-start | bytes 73736 | tf_op jit(solution)/shard_map/ppermute | solution.py:19
  101.9 3.1 collective-permute-start.3
  103.8 5.7 copy-start.32
  366.7 6.8 %copy-start.5 = (f32[8,32,32,8]{2,3,1,0:T(8,128)S(1)}, f32[8,32,32,8]{2,3,1,0:T(8,128)}, u32[]{:S(2)}) copy-start(f32[8,32,32,8]{2,3,1,0:T(8,128)} %broadcast_multiply_fusion) | copy-start | bytes 786436
  396.1 5.0 copy-start.8
  401.1 11.5 %copy-start.27 = (s32[8]{0:T(128)S(1)}, s32[8]{0:T(128)}, u32[]{:S(2)}) copy-start(s32[8]{0:T(128)} %copy-done.26) | copy-start | bytes 100
  401.1 11.5 %copy-start.29 = (pred[8]{0:T(512)(128)(4,1)S(1)}, pred[8]{0:T(512)(128)(4,1)}, u32[]{:S(2)}) copy-start(pred[8]{0:T(512)(128)(4,1)} %copy-done.28) | copy-start | bytes 28
  405.6 16.5 %copy-start.16 = (f32[8,32,256]{2,0,1:T(8,128)S(1)}, f32[8,32,256]{2,0,1:T(8,128)}, u32[]{:S(2)}) copy-start(f32[8,32,256]{2,0,1:T(8,128)} %copy-done.15) | copy-start | bytes 786436
  405.6 16.5 %copy-start.31 = (pred[256]{0:T(512)(128)(4,1)S(1)}, pred[256]{0:T(512)(128)(4,1)}, u32[]{:S(2)}) copy-start(pred[256]{0:T(512)(128)(4,1)} %copy-done.30) | copy-start | bytes 772
  405.7 5.4 collective-permute-start.4
  407.0 5.6 collective-permute-start.5
  413.0 8.1 %collective-permute-start.6 = (f32[3,8,1,256]{3,1,2,0:T(8,128)S(1)}, f32[3,8,1,256]{3,1,2,0:T(8,128)S(1)}, u32[]{:S(2)}, u32[]{:S(2)}) collective-permute-start(f32[3,8,1,256]{3,1,2,0:T(8,128)S(1)} %get-tuple-element.17), channel_id=1, source_target_pairs={{1,0},{2,1},{3,2},{4,3},{5,4},{6,5},{7,6},{9,8},{10,9},{11,10},{12... | collective-permute-start | bytes 73736 | tf_op jit(solution)/shard_map/ppermute | solution.py:19
  418.0 3.9 collective-permute-start.7
  (10 other events, 33.5 us)
Sparse Core Ops, SparseCore 0:
  111.1 246.7 all-reduce.4
where the time goes:
time: 599 us; the launch traced here: 589 us
  waiting for transfers between devices  252 us (42%)
  blocking collectives  154 us (26%)
  local copies, waits for them, and re-layouts  74.2 us (12%)
  matrix products  53.5 us (9%)
  starting transfers between devices  26.7 us (4%)
  between operations  17.2 us (3%)
  other arithmetic  11.9 us (2%)
    psum x1, waiting for transfers between devices, shards(): coarse_y = lax.psum(partial_y, ('gx', 'yz'))  247 us
    psum x1, blocking collectives, shards(): lax.psum((jnp.sum(weight * second * probe_field), jnp.sum(weight * probe_...  79.4 us
    psum x1, blocking collectives, shards(): lax.psum(jnp.sum(weight * remainder * remainder), ('gx', 'yz'))  74.6 us
    dot_general x15, matrix products, apply_along(): jnp.tensordot(blocks, matrix, axes=((spatial + 1,), (1,)), precision=lax....  50 us
    mul x6, local copies, waits for them, and re-layouts, element_apply(): viscosity * apply_along(mass_w * vector_grads[spatial - 1], derivative.T,...  16.6 us
    ppermute x4, starting transfers between devices, padded_2(): before = lax.ppermute(last, axis, up)  13.4 us
    ppermute x4, starting transfers between devices, padded_2(): after = lax.ppermute(first, axis, down)  13.3 us
  transfers between devices with their start and end apart: 9, of which 5 were waited for; matrix products, arithmetic and copies ran while one was open for 0% of the time, Pallas kernels for 0%

commit v1 on v0

v1 whole, which is shorter than its diff:
```python
import jax
import jax.numpy as jnp
import ml_dtypes
import numpy as np
from jax import lax
from jax.experimental import pallas as pl
from jax.experimental.pallas import tpu as pltpu
from jax.sharding import PartitionSpec as P

viscosity = 0.05
epsilon = 1e-06
MESH = pl.DeviceIdType.MESH
F32 = jnp.float32
BF16 = jnp.bfloat16
PLANE = 32
RING = 8


def tables():
    points = np.array(
        [
            -1.0,
            -0.8717401485096066,
            -0.5917001814331423,
            -0.2092992179024789,
            0.2092992179024789,
            0.5917001814331423,
            0.8717401485096066,
            1.0,
        ]
    )
    weights = np.array(
        [
            1.0 / 28.0,
            0.2107042271435061,
            0.3411226924835044,
            0.4124587946587038,
            0.4124587946587038,
            0.3411226924835044,
            0.2107042271435061,
            1.0 / 28.0,
        ]
    )
    differ = points[:, None] - points[None, :]
    positions = np.arange(8)
    differ[positions, positions] = 1.0
    barycentric = 1.0 / np.prod(differ, axis=1)
    derivative = barycentric[None, :] / barycentric[:, None] / differ
    derivative[positions, positions] = 0.0
    derivative[positions, positions] = -derivative.sum(axis=1)
    return derivative, weights


def halves(matrix):
    high = matrix.astype(ml_dtypes.bfloat16)
    low = (matrix - high.astype(np.float64)).astype(ml_dtypes.bfloat16)
    return high, low


def constants():
    derivative, weights = tables()
    stiff = viscosity * (derivative.T * weights[None, :]) @ derivative / weights[:, None]
    eye = np.eye
    along_x = np.kron(derivative, eye(32))
    along_y = np.kron(eye(32), derivative)
    spread_xy = np.kron(stiff, eye(32)) + np.kron(eye(32), stiff)
    left = np.concatenate([along_x, along_y, spread_xy], axis=0)
    right = np.concatenate([np.kron(eye(32), derivative.T), np.kron(eye(32), stiff.T)], axis=1)
    left = np.concatenate(halves(left), axis=1)
    right = np.concatenate(halves(right), axis=0)
    half = np.where((np.arange(8) == 0) | (np.arange(8) == 7), 0.5, 1.0)
    mass = np.tile(weights, 4)[:, None] * np.tile(weights, 32)[None, :]
    count = np.tile(half, 4)[:, None] * np.tile(half, 32)[None, :]
    return left, right, np.stack([mass, count]).astype(np.float32), weights


WEIGHTS = tables()[1]


def split(value):
    high = value.astype(BF16)
    return high, (value - high.astype(F32)).astype(BF16)


def kernel(
    slabs,
    columns,
    state_hbm,
    dir_hbm,
    xxt_hbm,
    ids_hbm,
    left_hbm,
    right_hbm,
    plane_hbm,
    sec_hbm,
    probe_hbm,
    scal_ref,
    state,
    direc,
    xxt,
    ids,
    left,
    right,
    plane,
    grads,
    lhs_out,
    rhs_out,
    local,
    image,
    local2,
    second,
    probe,
    onehot,
    cblock,
    part_y,
    recv_y,
    sum_b,
    recv_b,
    all_y,
    send_yl,
    send_yh,
    send_c,
    recv_xl,
    recv_xh,
    recv_yl,
    recv_yh,
    recv_c,
    row_a,
    recv_ra,
    row_b,
    recv_rb,
    in_sem,
    out_sem,
    halo_send,
    halo_recv,
    red_send,
    red_recv,
):
    gx, yz = lax.axis_index("gx"), lax.axis_index("yz")
    gz, px = gx // 4, gx % 4
    here = px * columns + yz

    def in_plane(k):
        other = lax.rem(here + k, PLANE)
        return (gz * 4 + other // columns, lax.rem(other, columns))

    def in_ring(k):
        return (lax.rem(gz + k, RING) * 4 + px, yz)

    def beside(dx, dy):
        return (lax.rem(gx + dx + slabs, slabs), lax.rem(yz + dy + columns, columns))

    loads = [
        pltpu.make_async_copy(src, dst, in_sem.at[i])
        for i, (src, dst) in enumerate(
            [
                (state_hbm, state),
                (left_hbm, left),
                (right_hbm, right),
                (dir_hbm, direc),
                (plane_hbm, plane),
                (ids_hbm, ids),
                (xxt_hbm, xxt),
            ]
        )
    ]
    for load in loads:
        load.start()

    barrier = pltpu.get_barrier_semaphore()
    greeted = [in_plane(k) for k in range(1, PLANE)]
    greeted += [in_ring(k) for k in range(1, RING)]
    greeted += [beside(dx, dy) for dx in (-1, 1) for dy in (-1, 0, 1)]
    for peer in greeted:
        pl.semaphore_signal(barrier, inc=1, device_id=peer, device_id_type=MESH)

    lane = lax.broadcasted_iota(jnp.int32, (1, 256), 1)
    from_next = ((lane % 8 == 7) & (lane != 255)).astype(F32)
    from_last = ((lane % 8 == 0) & (lane != 0)).astype(F32)
    inside = ((lane != 0) & (lane != 255)).astype(F32)
    wall_xl = jnp.where(gx == 0, 0.0, 1.0).astype(F32)
    wall_xh = jnp.where(gx == slabs - 1, 0.0, 1.0).astype(F32)
    wall_yl = jnp.where(yz == 0, 0.0, 1.0).astype(F32)
    wall_yh = jnp.where(yz == columns - 1, 0.0, 1.0).astype(F32)
    row8 = lax.broadcasted_iota(jnp.int32, (8, 1), 0)
    wall_x = jnp.where(row8 == 0, wall_xl, jnp.where(row8 == 7, wall_xh, 1.0))

    def fold_z(value):
        return (
            value * inside
            + pltpu.roll(value, 255, 1) * from_next
            + pltpu.roll(value, 1, 1) * from_last
        )

    def rows_of(p):
        return pl.ds(32 * p, 32)

    def get(ref, m, rows):
        return jnp.concatenate([ref[m, 0, rows, :], ref[m, 1, rows, :]], axis=1)

    def put(ref, m, rows, value):
        ref[m, 0, rows, :] = value[:, :128]
        ref[m, 1, rows, :] = value[:, 128:]

    def whole(ref, m, rows):
        return ref[m, rows, :]

    def products_left(value, rows, slot):
        high, low = split(value)
        ops = left[pl.ds(0, rows), :]
        lhs_out[slot, pl.ds(0, rows), :] = jnp.dot(
            jnp.concatenate([ops, ops[:, :256]], axis=1),
            jnp.concatenate([high, high, low], axis=0),
            preferred_element_type=F32,
        )
        return high, low

    def products_right(high, low, cols):
        ops = right[:, pl.ds(0, cols)]
        return jnp.dot(
            jnp.concatenate([high, high, low], axis=1),
            jnp.concatenate([ops, ops[:256]], axis=0),
            preferred_element_type=F32,
        )

    def apply_element(vector, take, m, target, slot):
        high, low = products_left(take(vector, m, pl.ds(0, 256)), 768, slot)
        rhs_out[slot] = products_right(high, low, 512)
        for p in (0, 7, 1, 2, 3, 4, 5, 6):
            rows = rows_of(p)
            total = lhs_out[slot, pl.ds(512 + 32 * p, 32), :] + rhs_out[slot, rows, pl.ds(256, 256)]
            total += state[0, rows, :] * lhs_out[slot, rows, :]
            total += state[1, rows, :] * lhs_out[slot, pl.ds(256 + 32 * p, 32), :]
            total += state[2, rows, :] * rhs_out[slot, rows, pl.ds(0, 256)]
            for k in range(3):
                total += take(vector, k, rows) * grads[m, k, rows, :]
            put(target, m, rows, total * (plane[0] * float(WEIGHTS[p])))

    def send(turn, index, src, dst, peer):
        pltpu.make_async_remote_copy(
            src_ref=src,
            dst_ref=dst,
            send_sem=halo_send.at[turn, index],
            recv_sem=halo_recv.at[turn, index],
            device_id=peer,
            device_id_type=MESH,
        ).start()

    def send_x(turn, source, m):
        send(turn, 0, source.at[m, :, pl.ds(224, 32), :], recv_xl.at[turn, m], beside(1, 0))
        send(turn, 1, source.at[m, :, pl.ds(0, 32), :], recv_xh.at[turn, m], beside(-1, 0))

    def send_y(turn, source):
        for m in range(3):
            low = get(source, m, pl.ds(0, 8, stride=32))
            high = get(source, m, pl.ds(31, 8, stride=32))
            send_yl[turn, m] = low
            send_yh[turn, m] = high
            send_c[turn, 0, pl.ds(m, 1), :] = low[0:1]
            send_c[turn, 1, pl.ds(m, 1), :] = high[0:1]
            send_c[turn, 2, pl.ds(m, 1), :] = low[7:8]
            send_c[turn, 3, pl.ds(m, 1), :] = high[7:8]
        send(turn, 2, send_yh.at[turn], recv_yl.at[turn], beside(0, 1))
        send(turn, 3, send_yl.at[turn], recv_yh.at[turn], beside(0, -1))
        for i, (dx, dy) in enumerate(((-1, -1), (-1, 1), (1, -1), (1, 1))):
            send(turn, 4 + i, send_c.at[turn, i], recv_c.at[turn, i], beside(dx, dy))

    def halo_refs(turn):
        refs = [recv_xl.at[turn], recv_xh.at[turn], recv_yl.at[turn], recv_yh.at[turn]]
        return refs + [recv_c.at[turn, i] for i in range(4)]

    def wait_halo(turn, sems):
        for i, ref in enumerate(halo_refs(turn)):
            pltpu.make_async_copy(ref, ref, sems.at[turn, i]).wait()

    def assemble(turn, source, target):
        for m in range(3):
            for p in range(8):
                value = get(source, m, rows_of(p))
                if p == 0:
                    value = (value + get(recv_xl.at[turn], m, pl.ds(0, 32))) * wall_xl
                if p == 7:
                    value = (value + get(recv_xh.at[turn], m, pl.ds(0, 32))) * wall_xh
                put(target, m, rows_of(p), fold_z(value))
            at_m = pl.ds(m, 1)
            low = recv_yl[turn, m]
            low += jnp.where(row8 == 0, recv_c[turn, 3, at_m, :], 0.0)
            low += jnp.where(row8 == 7, recv_c[turn, 1, at_m, :], 0.0)
            high = recv_yh[turn, m]
            high += jnp.where(row8 == 0, recv_c[turn, 2, at_m, :], 0.0)
            high += jnp.where(row8 == 7, recv_c[turn, 0, at_m, :], 0.0)
            first, last = pl.ds(0, 8, stride=32), pl.ds(31, 8, stride=32)
            put(target, m, first, (get(target, m, first) + fold_z(low) * wall_x) * wall_yl)
            put(target, m, last, (get(target, m, last) + fold_z(high) * wall_x) * wall_yh)
            for b in range(3):
                one, two = pl.ds(8 * b + 7, 8, stride=32), pl.ds(8 * b + 8, 8, stride=32)
                both = get(target, m, one) + get(target, m, two)
                put(target, m, one, both)
                put(target, m, two, both)

    def spread_out(phase, size, peer_of, src_of, dst_of):
        for k in range(1, size):
            pltpu.make_async_remote_copy(
                src_ref=src_of(k),
                dst_ref=dst_of(k),
                send_sem=red_send.at[phase],
                recv_sem=red_recv.at[phase],
                device_id=peer_of(k),
                device_id_type=MESH,
            ).start()

    def wait_bytes(ref, sem):
        pltpu.make_async_copy(ref, ref, sem).wait()

    loads[0].wait()
    loads[1].wait()
    loads[2].wait()
    loads[3].wait()
    loads[4].wait()
    for m in range(3):
        slot = m % 2
        high, low = products_left(state[m], 512, slot)
        grads[m, 2] = products_right(high, low, 256)
        grads[m, 0] = lhs_out[slot, pl.ds(0, 256), :]
        grads[m, 1] = lhs_out[slot, pl.ds(256, 256), :]
    for m in range(3):
        apply_element(direc, whole, m, local, m % 2)
        if m == 0:
            pl.semaphore_wait(barrier, len(greeted))
        send_x(0, local, m)
    send_y(0, local)

    loads[5].wait()
    elem = lax.broadcasted_iota(jnp.int32, (128, 1024), 0)
    spot = lax.broadcasted_iota(jnp.int32, (128, 1024), 1)
    wide = jnp.dot(
        jnp.broadcast_to(ids[...].astype(F32), (8, 128)).astype(BF16),
        (spot // 8 == elem).astype(F32).astype(BF16),
        preferred_element_type=F32,
    )
    for t in range(4):
        row = (lax.broadcasted_iota(jnp.int32, (8, 1024), 0) + 8 * t).astype(F32)
        onehot[pl.ds(8 * t, 8), :] = jnp.where(jnp.abs(wide - row) < 0.5, 1.0, 0.0)
    loads[6].wait()

    wait_halo(0, halo_recv)
    assemble(0, local, image)

    coarse = []
    for m in range(3):
        total = get(image, m, rows_of(0)) * float(WEIGHTS[0])
        for p in range(1, 8):
            total += get(image, m, rows_of(p)) * float(WEIGHTS[p])
        total *= plane[0]
        acc = jnp.zeros((32, 256), F32)
        for b in range(4):
            line = jnp.sum(total[8 * b : 8 * b + 8], axis=0, keepdims=True)
            acc += onehot[:, pl.ds(256 * b, 256)] * line
        coarse.append(jnp.sum(acc, axis=1, keepdims=True))
    for j in range(PLANE):
        block = xxt[:, pl.ds(256 * j, 256)]
        for m in range(3):
            part_y[j, pl.ds(m, 1), :] = jnp.sum(block * coarse[m], axis=0, keepdims=True)

    spread_out(
        0,
        PLANE,
        in_plane,
        lambda k: part_y.at[lax.rem(here + k, PLANE)],
        lambda k: recv_y.at[k - 1],
    )
    apply_element(image, get, 0, local2, 0)
    wait_bytes(recv_y, red_recv.at[0])
    total = part_y[here]
    for k in range(PLANE - 1):
        total += recv_y[k]
    sum_b[...] = total
    spread_out(1, RING, in_ring, lambda k: sum_b, lambda k: recv_b.at[k - 1])
    apply_element(image, get, 1, local2, 1)
    wait_bytes(recv_b, red_recv.at[1])
    total = sum_b[...]
    for k in range(RING - 1):
        total += recv_b[k]
    all_y[here] = total
    spread_out(2, PLANE, in_plane, lambda k: all_y.at[here], lambda k: all_y.at[here])
    apply_element(image, get, 2, local2, 0)
    wait_bytes(all_y.at[pl.ds(0, PLANE - 1)], red_recv.at[2])

    sums = [jnp.zeros((32, 256), F32) for _ in range(3)]
    for j in range(PLANE):
        block = xxt[:, pl.ds(256 * j, 256)]
        for m in range(3):
            sums[m] += block * all_y[j, pl.ds(m, 1), :]
    for m in range(3):
        column = jnp.sum(sums[m], axis=1, keepdims=True)
        for b in range(4):
            line = jnp.sum(onehot[:, pl.ds(256 * b, 256)] * column, axis=0, keepdims=True)
            cblock[m, pl.ds(8 * b, 8), :] = jnp.broadcast_to(line, (8, 256))

    def add_correction(m, p):
        rows = rows_of(p)
        total = cblock[0] * grads[m, 0, rows, :]
        total += cblock[1] * grads[m, 1, rows, :]
        total += cblock[2] * grads[m, 2, rows, :]
        put(local2, m, rows, get(local2, m, rows) + total * (plane[0] * float(WEIGHTS[p])))

    for m in range(3):
        add_correction(m, 0)
        add_correction(m, 7)
        send_x(1, local2, m)
    for m in range(3):
        for p in range(1, 7):
            add_correction(m, p)
    send_y(1, local2)
    for m in range(3):
        for p in range(8):
            probe[m, rows_of(p), :] = get(image, m, rows_of(p)) + cblock[m]
    probe_out = pltpu.make_async_copy(probe, probe_hbm, out_sem.at[0])
    probe_out.start()
    wait_halo(1, halo_recv)
    assemble(1, local2, second)
    second_out = [
        pltpu.make_async_copy(
            second.at[:, h], sec_hbm.at[:, :, pl.ds(128 * h, 128)], out_sem.at[1 + h]
        )
        for h in range(2)
    ]
    for out in second_out:
        out.start()

    def both_sums(one, two):
        results = []
        for value in (one, two):
            results.append(jnp.sum(jnp.sum(value * plane[1], axis=0, keepdims=True), axis=1, keepdims=True))
        return results

    acc_sp, acc_pp = jnp.zeros((32, 256), F32), jnp.zeros((32, 256), F32)
    for p in range(8):
        sp, pp = jnp.zeros((32, 256), F32), jnp.zeros((32, 256), F32)
        for m in range(3):
            pr = probe[m, rows_of(p), :]
            sp += get(second, m, rows_of(p)) * pr
            pp += pr * pr
        scale = 0.5 if p in (0, 7) else 1.0
        acc_sp += scale * sp
        acc_pp += scale * pp
    sp, pp = both_sums(acc_sp, acc_pp)
    own = jnp.where(pp > 0, sp / jnp.where(pp > 0, pp, 1.0), 0.0)
    acc_q, acc_rr = jnp.zeros((32, 256), F32), jnp.zeros((32, 256), F32)
    for p in range(8):
        q, rr = jnp.zeros((32, 256), F32), jnp.zeros((32, 256), F32)
        for m in range(3):
            pr = probe[m, rows_of(p), :]
            rest = get(second, m, rows_of(p)) - own * pr
            q += rest * pr
            rr += rest * rest
        scale = 0.5 if p in (0, 7) else 1.0
        acc_q += scale * q
        acc_rr += scale * rr
    q, rr = both_sums(acc_q, acc_rr)

    lane128 = lax.broadcasted_iota(jnp.int32, (1, 128), 1)

    def pack(one, two, three, four):
        rest = jnp.where(lane128 < 96, three, four)
        return jnp.where(lane128 < 32, one, jnp.where(lane128 < 64, two, rest))

    def unpack(rows):
        return rows, pltpu.roll(rows, 96, 1), pltpu.roll(rows, 64, 1), pltpu.roll(rows, 32, 1)

    def total_of(rows):
        return jnp.sum(rows, axis=0, keepdims=True)

    def gather_rows(own_row, ref, count):
        return jnp.concatenate([own_row] + [ref[k] for k in range(count)], axis=0)

    message = pack(own, q, pp, rr)
    row_a[...] = message
    spread_out(3, PLANE, in_plane, lambda k: row_a, lambda k: recv_ra.at[k - 1])
    wait_bytes(recv_ra, red_recv.at[3])
    own, q, pp, rr = unpack(gather_rows(message, recv_ra, PLANE - 1))
    mean_sp, mean_pp = total_of(q + own * pp), total_of(pp)
    merged = jnp.where(mean_pp > 0, mean_sp / jnp.where(mean_pp > 0, mean_pp, 1.0), 0.0)
    away = own - merged
    q, rr = total_of(q + away * pp), total_of(rr + 2.0 * away * q + away * away * pp)
    message = pack(merged, pltpu.roll(q, 32, 1), pltpu.roll(mean_pp, 64, 1), pltpu.roll(rr, 96, 1))
    row_b[...] = message
    spread_out(4, RING, in_ring, lambda k: row_b, lambda k: recv_rb.at[k - 1])
    wait_bytes(recv_rb, red_recv.at[4])
    own, q, pp, rr = unpack(gather_rows(message, recv_rb, RING - 1))
    weight_total = 343.0 * 128 * slabs * columns
    mean_sp, mean_pp = total_of(q + own * pp) / weight_total, total_of(pp) / weight_total
    coef = mean_sp / (mean_pp + epsilon)
    away = own - coef
    rest_mean = total_of(rr + 2.0 * away * q + away * away * pp) / weight_total
    rms = jnp.sqrt(jnp.maximum(rest_mean, 0.0) + epsilon)
    scal_ref[...] = jnp.concatenate([coef, rms, 1.0 / rms, jnp.zeros((5, 128), F32)], axis=0)

    wait_halo(0, halo_send)
    wait_halo(1, halo_send)
    wait_bytes(recv_y, red_send.at[0])
    wait_bytes(recv_b, red_send.at[1])
    wait_bytes(all_y.at[pl.ds(0, PLANE - 1)], red_send.at[2])
    wait_bytes(recv_ra, red_send.at[3])
    wait_bytes(recv_rb, red_send.at[4])
    probe_out.wait()
    for out in second_out:
        out.wait()


def shards(slabs, columns, state, direction, xxt_rows, coarse_ids):
    shape = state.shape
    left, right, plane, _ = constants()
    vmem = pltpu.VMEM
    field = (3, 256, 256)
    halved = (3, 2, 256, 128)

    def body(*refs):
        kernel(slabs, columns, *refs)

    anywhere = pl.BlockSpec(memory_space=pl.ANY)
    sec, probe, scal = pl.pallas_call(
        body,
        out_shape=(
            jax.ShapeDtypeStruct(field, F32),
            jax.ShapeDtypeStruct(field, F32),
            jax.ShapeDtypeStruct((8, 128), F32),
        ),
        in_specs=[anywhere] * 7,
        out_specs=(anywhere, anywhere, pl.BlockSpec(memory_space=vmem)),
        scratch_shapes=[
            vmem(field, F32),
            vmem(field, F32),
            vmem((32, 8192), F32),
            vmem((1, 128), jnp.int32),
            vmem((768, 512), BF16),
            vmem((512, 512), BF16),
            vmem((2, 32, 256), F32),
            vmem((3, 3, 256, 256), F32),
            vmem((2, 768, 256), F32),
            vmem((2, 256, 512), F32),
            vmem(halved, F32),
            vmem(halved, F32),
            vmem(halved, F32),
            vmem(halved, F32),
            vmem(field, F32),
            vmem((32, 1024), F32),
            vmem((3, 32, 256), F32),
            vmem((PLANE, 4, 256), F32),
            vmem((PLANE - 1, 4, 256), F32),
            vmem((4, 256), F32),
            vmem((RING - 1, 4, 256), F32),
            vmem((PLANE, 4, 256), F32),
            vmem((2, 3, 8, 256), F32),
            vmem((2, 3, 8, 256), F32),
            vmem((2, 4, 4, 256), F32),
            vmem((2, 3, 2, 32, 128), F32),
            vmem((2, 3, 2, 32, 128), F32),
            vmem((2, 3, 8, 256), F32),
            vmem((2, 3, 8, 256), F32),
            vmem((2, 4, 4, 256), F32),
            vmem((1, 128), F32),
            vmem((PLANE - 1, 1, 128), F32),
            vmem((1, 128), F32),
            vmem((RING - 1, 1, 128), F32),
            pltpu.SemaphoreType.DMA((7,)),
            pltpu.SemaphoreType.DMA((3,)),
            pltpu.SemaphoreType.DMA((2, 8)),
            pltpu.SemaphoreType.DMA((2, 8)),
            pltpu.SemaphoreType.DMA((5,)),
            pltpu.SemaphoreType.DMA((5,)),
        ],
        compiler_params=pltpu.CompilerParams(
            collective_id=0, has_side_effects=True, vmem_limit_bytes=40 * 1024 * 1024
        ),
        name="jacobian_products",
    )(
        state.reshape(field),
        direction.reshape(field),
        xxt_rows,
        coarse_ids,
        jnp.asarray(left),
        jnp.asarray(right),
        jnp.asarray(plane),
    )
    next_basis = (sec - scal[0, 0] * probe) * scal[2, 0]
    return next_basis.reshape(shape), scal[:2, 0]


def solution(mesh):
    slabs, columns = mesh.shape["gx"], mesh.shape["yz"]

    def local_shards(*args):
        return shards(slabs, columns, *args)

    return jax.shard_map(
        local_shards,
        mesh=mesh,
        in_specs=(
            P(None, "gx", "yz", None),
            P(None, "gx", "yz", None),
            P(("gx", "yz"), None),
            P(("gx", "yz"), None),
        ),
        out_specs=(P(None, "gx", "yz", None), P()),
        check_vma=False,
    )
```

time: 599 us -> 61.2 us (0.10); the launches traced: 589 us -> 60.8 us
  waiting for transfers between devices: 252 us -> 0 us
  blocking collectives: 154 us -> 0 us
  local copies, waits for them, and re-layouts: 74.2 us -> 8.37 us
  matrix products: 53.5 us -> 0 us
  Pallas kernels: 0 us -> 49.6 us
  starting transfers between devices: 26.7 us -> 0 us
  between operations: 17.2 us -> 0.65 us
  other arithmetic: 11.9 us -> 2.23 us
    psum x1 -> x0, waiting for transfers between devices: 247 us -> none  [shards(): coarse_y = lax.psum(partial_y, ('gx', 'yz'))]
    psum x2 -> x0, blocking collectives: 154 us -> none  [the longest x1 79.4 us: shards(): lax.psum((jnp.sum(weight * second * probe_field), jnp.sum(weight * probe_...]
    dot_general x19 -> x0, matrix products: 53.5 us -> none  [the longest x15 50 us: apply_along(): jnp.tensordot(blocks, matrix, axes=((spatial + 1,), (1,)), precision=lax....]
    pallas_call x0 -> x1, Pallas kernels: none -> 49.6 us  [shards(): pl.pallas_call(body, out_shape=(jax.ShapeDtypeStruct(field, F32), jax.Sha...]
    ppermute x8 -> x0, starting transfers between devices: 26.7 us -> none  [the longest x4 13.4 us: padded_2(): before = lax.ppermute(last, axis, up)]
    mul x18 -> x0, local copies, waits for them, and re-layouts: 23.3 us -> none  [the longest x6 16.6 us: element_apply(): viscosity * apply_along(mass_w * vector_grads[spatial - 1], derivative.T,...]
    reshape x8 -> x0, local copies, waits for them, and re-layouts: 20.2 us -> none  [the longest x3 11 us: apply_along(): tensor.reshape(full_shape[:spatial] + (full_shape[spatial] // 8, 8) + ful...]
    dot_general x3 -> x0, local copies, waits for them, and re-layouts: 11.1 us -> none  [apply_along(): jnp.tensordot(blocks, matrix, axes=((spatial + 1,), (1,)), precision=lax....]
  transfers between devices with their start and end apart: 9 -> 0, of which waited for: 5 -> 0; matrix products, arithmetic and copies ran while one was open for 0% -> 0% of each run, Pallas kernels for 0% -> 0%
where the time goes in v1:
time: 61.2 us; the launch traced here: 60.8 us
  Pallas kernels  49.6 us (81%)
  local copies, waits for them, and re-layouts  8.37 us (14%)
  other arithmetic  2.23 us (4%)
  between operations  0.65 us (1%)
    pallas_call x1, Pallas kernels, shards(): pl.pallas_call(body, out_shape=(jax.ShapeDtypeStruct(field, F32), jax.Sha...  49.6 us
    unnamed x14, local copies, waits for them, and re-layouts  7.15 us
    mul x1, other arithmetic, shards(): next_basis = (sec - scal[0, 0] * probe) * scal[2, 0]  2.23 us

profile of v1, /device:TPU:1, one launch (start us, length us, event | category | flops | bytes accessed | tf_op | source)
XLA Modules:
  0.0 60.8 jit_solution(18336940329988512808)
XLA Ops:
  0.6 0.0 copy-start.6
  0.6 0.6 %copy-done.6 = s32[1,128]{1,0:T(1,128)S(1)} copy-done((s32[1,128]{1,0:T(1,128)S(1)}, s32[1,128]{1,0:T(1,128)}, u32[]{:S(2)}) %copy-start.6) | copy-done | bytes 536
  1.3 0.0 copy-start
  1.3 1.2 %copy-done = f32[32,8192]{1,0:T(8,128)S(1)} copy-done((f32[32,8192]{1,0:T(8,128)S(1)}, f32[32,8192]{1,0:T(8,128)}, u32[]{:S(2)}) %copy-start) | copy-done | bytes 1048600
  2.5 0.0 copy-start.1
  2.5 1.1 %copy-done.1 = f32[3,8,32,256]{3,2,1,0:T(8,128)S(1)} copy-done((f32[3,8,32,256]{3,2,1,0:T(8,128)S(1)}, f32[3,8,32,256]{3,2,1,0:T(8,128)}, u32[]{:S(2)}) %copy-start.1) | copy-done | bytes 786456
  3.6 0.0 copy-start.2
  3.6 1.1 %copy-done.2 = f32[3,8,32,256]{3,2,1,0:T(8,128)S(1)} copy-done((f32[3,8,32,256]{3,2,1,0:T(8,128)S(1)}, f32[3,8,32,256]{3,2,1,0:T(8,128)}, u32[]{:S(2)}) %copy-start.2) | copy-done | bytes 786456
  4.8 0.0 copy-start.3
  4.8 1.1 %copy-done.3 = bf16[768,512]{1,0:T(8,128)(2,1)S(1)} copy-done((bf16[768,512]{1,0:T(8,128)(2,1)S(1)}, bf16[768,512]{1,0:T(8,128)(2,1)}, u32[]{:S(2)}) %copy-start.3) | copy-done | bytes 786456
  5.9 0.0 copy-start.4
  5.9 1.0 %copy-done.4 = bf16[512,512]{1,0:T(8,128)(2,1)S(1)} copy-done((bf16[512,512]{1,0:T(8,128)(2,1)S(1)}, bf16[512,512]{1,0:T(8,128)(2,1)}, u32[]{:S(2)}) %copy-start.4) | copy-done | bytes 524312
  7.0 0.0 copy-start.5
  7.0 0.8 %copy-done.5 = f32[2,32,256]{2,1,0:T(8,128)S(1)} copy-done((f32[2,32,256]{2,1,0:T(8,128)S(1)}, f32[2,32,256]{2,1,0:T(8,128)}, u32[]{:S(2)}) %copy-start.5) | copy-done | bytes 65560
  7.8 49.6 %jacobian_products.1 = (f32[3,256,256]{2,1,0:T(8,128)S(1)}, f32[3,256,256]{2,1,0:T(8,128)S(1)}, f32[8,128]{1,0:T(8,128)S(1)}) custom-call(f32[3,256,256]{2,1,0:T(8,128)S(1)} %bitcast.5, f32[3,256,256]{2,1,0:T(8,128)S(1)} %bitcast.6, f32[32,8192]{1,0:T(8,128)S(1)} %copy-done, s32[1,128]{1,0:T(1,128)S(1)} %copy-done.6, bf16[768,512]{1,0:T(8,128)(2,1)S(1)} %copy-done.3, ...), custom_call_target="tpu_custom_call" | custom-call | tf_op jit(solution)/shard_map/jacobian_products/pallas_call | solution.py:522
  57.4 0.6 %slice_reduce_fusion = f32[2]{0:T(128)} fusion(f32[8,128]{1,0:T(8,128)S(1)} %get-tuple-element.6), kind=kLoop, calls=%fused_computation.1 | loop fusion | bytes 16 | tf_op jit(solution)/shard_map/slice | solution.py:587
  58.0 0.6 fusion
  58.6 2.2 %subtract_multiply_fusion = f32[3,256,256]{2,1,0:T(8,128)} fusion(f32[3,256,256]{2,1,0:T(8,128)S(1)} %get-tuple-element.5, f32[3,256,256]{2,1,0:T(8,128)S(1)} %get-tuple-element.7, f32[]{:T(128)} %bitcast.3, f32[]{:T(128)} %bitcast.2), kind=kLoop, calls=%fused_computation | loop fusion | flops 589824 | bytes 2359304 | tf_op jit(solution)/shard_map/mul | solution.py:586
Async XLA Ops:
  0.6 0.7 %copy-start.6 = (s32[1,128]{1,0:T(1,128)S(1)}, s32[1,128]{1,0:T(1,128)}, u32[]{:S(2)}) copy-start(s32[1,128]{1,0:T(1,128)} %refs_3_.1) | copy-start | bytes 1540
  1.3 1.2 %copy-start = (f32[32,8192]{1,0:T(8,128)S(1)}, f32[32,8192]{1,0:T(8,128)}, u32[]{:S(2)}) copy-start(f32[32,8192]{1,0:T(8,128)} %refs_2_.1) | copy-start | bytes 3145732
  2.5 1.1 %copy-start.1 = (f32[3,8,32,256]{3,2,1,0:T(8,128)S(1)}, f32[3,8,32,256]{3,2,1,0:T(8,128)}, u32[]{:S(2)}) copy-start(f32[3,8,32,256]{3,2,1,0:T(8,128)} %param.7) | copy-start | bytes 2359300
  3.6 1.1 %copy-start.2 = (f32[3,8,32,256]{3,2,1,0:T(8,128)S(1)}, f32[3,8,32,256]{3,2,1,0:T(8,128)}, u32[]{:S(2)}) copy-start(f32[3,8,32,256]{3,2,1,0:T(8,128)} %param.8) | copy-start | bytes 2359300
  4.8 1.1 %copy-start.3 = (bf16[768,512]{1,0:T(8,128)(2,1)S(1)}, bf16[768,512]{1,0:T(8,128)(2,1)}, u32[]{:S(2)}) copy-start(bf16[768,512]{1,0:T(8,128)(2,1)} %constant.6.clone.refs_4_) | copy-start | bytes 2359300
  5.9 1.0 %copy-start.4 = (bf16[512,512]{1,0:T(8,128)(2,1)S(1)}, bf16[512,512]{1,0:T(8,128)(2,1)}, u32[]{:S(2)}) copy-start(bf16[512,512]{1,0:T(8,128)(2,1)} %constant.7.clone.refs_5_) | copy-start | bytes 1572868
  7.0 0.8 %copy-start.5 = (f32[2,32,256]{2,1,0:T(8,128)S(1)}, f32[2,32,256]{2,1,0:T(8,128)}, u32[]{:S(2)}) copy-start(f32[2,32,256]{2,1,0:T(8,128)} %constant.8.clone.refs_6_) | copy-start | bytes 196612

commit v2 on v1

--- a/solution.py
+++ b/solution.py
@@ -14,6 +14,7 @@
 BF16 = jnp.bfloat16
 PLANE = 32
 RING = 8
+VMEM_LIMIT = 60 * 1024 * 1024
 
 
 def tables():
@@ -51,6 +52,23 @@
     return derivative, weights
 
 
+GROUPS = ((0, 64, (0, 7)), (192, 192, (1, 2, 3, 4, 5, 6)))
+DIMS = {"z": 8, "x": 4, "y": 4, "c": 2}
+
+
+def offsets(names):
+    found = []
+    for k in range(1, int(np.prod([DIMS[n] for n in names]))):
+        place, hops, rest = {}, 0.0, k
+        for n in reversed(names):
+            place[n] = rest % DIMS[n]
+            rest //= DIMS[n]
+            near = min(place[n], DIMS[n] - place[n])
+            hops += 0.25 * near if n == "c" else near
+        found.append((-hops, k, place))
+    return [(k, place) for _, k, place in sorted(found, key=lambda item: item[:2])]
+
+
 def halves(matrix):
     high = matrix.astype(ml_dtypes.bfloat16)
     low = (matrix - high.astype(np.float64)).astype(ml_dtypes.bfloat16)
@@ -64,7 +82,13 @@
     along_x = np.kron(derivative, eye(32))
     along_y = np.kron(eye(32), derivative)
     spread_xy = np.kron(stiff, eye(32)) + np.kron(eye(32), stiff)
-    left = np.concatenate([along_x, along_y, spread_xy], axis=0)
+    left = [
+        op[32 * plane : 32 * plane + 32]
+        for _, _, planes in GROUPS
+        for op in (along_x, along_y, spread_xy)
+        for plane in planes
+    ]
+    left = np.concatenate(left, axis=0)
     right = np.concatenate([np.kron(eye(32), derivative.T), np.kron(eye(32), stiff.T)], axis=1)
     left = np.concatenate(halves(left), axis=1)
     right = np.concatenate(halves(right), axis=0)
@@ -102,6 +126,8 @@
     left,
     right,
     plane,
+    highs,
+    lows,
     grads,
     lhs_out,
     rhs_out,
@@ -127,8 +153,6 @@
     recv_c,
     row_a,
     recv_ra,
-    row_b,
-    recv_rb,
     in_sem,
     out_sem,
     halo_send,
@@ -140,36 +164,28 @@
     gz, px = gx // 4, gx % 4
     here = px * columns + yz
 
-    def in_plane(k):
-        other = lax.rem(here + k, PLANE)
-        return (gz * 4 + other // columns, lax.rem(other, columns))
-
-    def in_ring(k):
-        return (lax.rem(gz + k, RING) * 4 + px, yz)
+    def peer_at(place):
+        z = lax.rem(gz + place.get("z", 0), 8)
+        x = lax.rem(px + place.get("x", 0), 4)
+        y = lax.rem(yz // 2 + place.get("y", 0), 4)
+        c = lax.rem(yz % 2 + place.get("c", 0), 2)
+        return (z * 4 + x, y * 2 + c)
+
+    in_plane, in_ring, everyone = offsets("xyc"), offsets("z"), offsets("zxyc")
 
     def beside(dx, dy):
         return (lax.rem(gx + dx + slabs, slabs), lax.rem(yz + dy + columns, columns))
 
-    loads = [
-        pltpu.make_async_copy(src, dst, in_sem.at[i])
-        for i, (src, dst) in enumerate(
-            [
-                (state_hbm, state),
-                (left_hbm, left),
-                (right_hbm, right),
-                (dir_hbm, direc),
-                (plane_hbm, plane),
-                (ids_hbm, ids),
-                (xxt_hbm, xxt),
-            ]
-        )
-    ]
-    for load in loads:
+    pairs = [(left_hbm, left), (state_hbm.at[0], state.at[0]), (right_hbm, right)]
+    pairs += [(state_hbm.at[m], state.at[m]) for m in (1, 2)]
+    pairs += [(dir_hbm.at[m], direc.at[m]) for m in range(3)]
+    pairs += [(plane_hbm, plane), (ids_hbm, ids), (xxt_hbm, xxt)]
+    loads = [pltpu.make_async_copy(src, dst, in_sem.at[i]) for i, (src, dst) in enumerate(pairs)]
+    for load in loads[:-1]:
         load.start()
 
     barrier = pltpu.get_barrier_semaphore()
-    greeted = [in_plane(k) for k in range(1, PLANE)]
-    greeted += [in_ring(k) for k in range(1, RING)]
+    greeted = [peer_at(place) for _, place in in_plane + in_ring]
     greeted += [beside(dx, dy) for dx in (-1, 1) for dy in (-1, 0, 1)]
     for peer in greeted:
         pl.semaphore_signal(barrier, inc=1, device_id=peer, device_id_type=MESH)
@@ -205,36 +221,67 @@
     def whole(ref, m, rows):
         return ref[m, rows, :]
 
-    def products_left(value, rows, slot):
+    def split_into(value, which, m):
         high, low = split(value)
-        ops = left[pl.ds(0, rows), :]
-        lhs_out[slot, pl.ds(0, rows), :] = jnp.dot(
+        highs[which, m] = high
+        lows[which, m] = low
+
+    def products_left(which, m, g, count):
+        first, rows, _ = GROUPS[g]
+        ops = left[pl.ds(first, rows * count), :]
+        high, low = highs[which, m], lows[which, m]
+        return jnp.dot(
             jnp.concatenate([ops, ops[:, :256]], axis=1),
             jnp.concatenate([high, high, low], axis=0),
             preferred_element_type=F32,
         )
-        return high, low
-
-    def products_right(high, low, cols):
+
+    def products_right(which, m, g, cols):
         ops = right[:, pl.ds(0, cols)]
+        high, low = (
+            jnp.concatenate([ref[which, m, rows_of(p), :] for p in GROUPS[g][2]], axis=0)
+            for ref in (highs, lows)
+        )
         return jnp.dot(
             jnp.concatenate([high, high, low], axis=1),
             jnp.concatenate([ops, ops[:256]], axis=0),
             preferred_element_type=F32,
         )
 
-    def apply_element(vector, take, m, target, slot):
-        high, low = products_left(take(vector, m, pl.ds(0, 256)), 768, slot)
-        rhs_out[slot] = products_right(high, low, 512)
-        for p in (0, 7, 1, 2, 3, 4, 5, 6):
+    def state_gradients(m, g):
+        _, size, planes = GROUPS[g]
+        by_left = products_left(0, m, g, 2)
+        by_right = products_right(0, m, g, 256)
+        for i, p in enumerate(planes):
+            grads[m, 0, rows_of(p), :] = by_left[32 * i : 32 * i + 32]
+            grads[m, 1, rows_of(p), :] = by_left[size + 32 * i : size + 32 * i + 32]
+            grads[m, 2, rows_of(p), :] = by_right[32 * i : 32 * i + 32]
+
+    def multiply(which, m, g):
+        first, size, planes = GROUPS[g]
+        lhs_out[m, pl.ds(first, 3 * size), :] = products_left(which, m, g, 3)
+        by_right = products_right(which, m, g, 512)
+        for i, p in enumerate(planes):
+            rhs_out[m, rows_of(p), :] = by_right[32 * i : 32 * i + 32]
+
+    def combine(vector, take, m, g, target):
+        first, size, planes = GROUPS[g]
+        for i, p in enumerate(planes):
             rows = rows_of(p)
-            total = lhs_out[slot, pl.ds(512 + 32 * p, 32), :] + rhs_out[slot, rows, pl.ds(256, 256)]
-            total += state[0, rows, :] * lhs_out[slot, rows, :]
-            total += state[1, rows, :] * lhs_out[slot, pl.ds(256 + 32 * p, 32), :]
-            total += state[2, rows, :] * rhs_out[slot, rows, pl.ds(0, 256)]
+            at = [pl.ds(first + size * op + 32 * i, 32) for op in range(3)]
+            total = lhs_out[m, at[2], :] + rhs_out[m, rows, pl.ds(256, 256)]
+            total += state[0, rows, :] * lhs_out[m, at[0], :]
+            total += state[1, rows, :] * lhs_out[m, at[1], :]
+            total += state[2, rows, :] * rhs_out[m, rows, pl.ds(0, 256)]
             for k in range(3):
                 total += take(vector, k, rows) * grads[m, k, rows, :]
             put(target, m, rows, total * (plane[0] * float(WEIGHTS[p])))
+
+    def apply_to_image(m):
+        split_into(get(image, m, pl.ds(0, 256)), 1, m)
+        for g in range(2):
+            multiply(1, m, g)
+            combine(image, get, m, g, local2)
 
     def send(turn, index, src, dst, peer):
         pltpu.make_async_remote_copy(
@@ -273,15 +320,17 @@
         for i, ref in enumerate(halo_refs(turn)):
             pltpu.make_async_copy(ref, ref, sems.at[turn, i]).wait()
 
-    def assemble(turn, source, target):
+    def assemble_inside(source, target):
         for m in range(3):
-            for p in range(8):
-                value = get(source, m, rows_of(p))
-                if p == 0:
-                    value = (value + get(recv_xl.at[turn], m, pl.ds(0, 32))) * wall_xl
-                if p == 7:
-                    value = (value + get(recv_xh.at[turn], m, pl.ds(0, 32))) * wall_xh
-                put(target, m, rows_of(p), fold_z(value))
+            for p in range(1, 7):
+                put(target, m, rows_of(p), fold_z(get(source, m, rows_of(p))))
+
+    def assemble_faces(turn, source, target):
+        for m in range(3):
+            value = get(source, m, rows_of(0)) + get(recv_xl.at[turn], m, pl.ds(0, 32))
+            put(target, m, rows_of(0), fold_z(value * wall_xl))
+            value = get(source, m, rows_of(7)) + get(recv_xh.at[turn], m, pl.ds(0, 32))
+            put(target, m, rows_of(7), fold_z(value * wall_xh))
             at_m = pl.ds(m, 1)
             low = recv_yl[turn, m]
             low += jnp.where(row8 == 0, recv_c[turn, 3, at_m, :], 0.0)
@@ -298,14 +347,15 @@
                 put(target, m, one, both)
                 put(target, m, two, both)
 
-    def spread_out(phase, size, peer_of, src_of, dst_of):
-        for k in range(1, size):
+    def spread_out(phase, places, src_of, dst_of):
+        for k, place in places:
+            peer = peer_at(place)
             pltpu.make_async_remote_copy(
-                src_ref=src_of(k),
+                src_ref=src_of(peer),
                 dst_ref=dst_of(k),
                 send_sem=red_send.at[phase],
                 recv_sem=red_recv.at[phase],
-                device_id=peer_of(k),
+                device_id=peer,
                 device_id_type=MESH,
             ).start()
 
@@ -313,24 +363,31 @@
         pltpu.make_async_copy(ref, ref, sem).wait()
 
     loads[0].wait()
-    loads[1].wait()
-    loads[2].wait()
-    loads[3].wait()
-    loads[4].wait()
-    for m in range(3):
-        slot = m % 2
-        high, low = products_left(state[m], 512, slot)
-        grads[m, 2] = products_right(high, low, 256)
-        grads[m, 0] = lhs_out[slot, pl.ds(0, 256), :]
-        grads[m, 1] = lhs_out[slot, pl.ds(256, 256), :]
-    for m in range(3):
-        apply_element(direc, whole, m, local, m % 2)
+    for m in range(3):
+        loads[(1, 3, 4)[m]].wait()
+        split_into(state[m], 0, m)
+        if m == 0:
+            loads[2].wait()
+        state_gradients(m, 0)
+    for m in range(3):
+        loads[5 + m].wait()
+        split_into(direc[m], 1, m)
+        multiply(1, m, 0)
+    loads[8].wait()
+    for m in range(3):
+        combine(direc, whole, m, 0, local)
         if m == 0:
             pl.semaphore_wait(barrier, len(greeted))
         send_x(0, local, m)
+    loads[10].start()
+    for m in range(3):
+        state_gradients(m, 1)
+        multiply(1, m, 1)
+        combine(direc, whole, m, 1, local)
     send_y(0, local)
-
-    loads[5].wait()
+    assemble_inside(local, image)
+
+    loads[9].wait()
     elem = lax.broadcasted_iota(jnp.int32, (128, 1024), 0)
     spot = lax.broadcasted_iota(jnp.int32, (128, 1024), 1)
     wide = jnp.dot(
@@ -341,10 +398,10 @@
     for t in range(4):
         row = (lax.broadcasted_iota(jnp.int32, (8, 1024), 0) + 8 * t).astype(F32)
         onehot[pl.ds(8 * t, 8), :] = jnp.where(jnp.abs(wide - row) < 0.5, 1.0, 0.0)
-    loads[6].wait()
+    loads[10].wait()
 
     wait_halo(0, halo_recv)
-    assemble(0, local, image)
+    assemble_faces(0, local, image)
 
     coarse = []
     for m in range(3):
@@ -362,28 +419,30 @@
         for m in range(3):
             part_y[j, pl.ds(m, 1), :] = jnp.sum(block * coarse[m], axis=0, keepdims=True)
 
+    def place_in_plane(peer):
+        return lax.rem(peer[0], 4) * columns + peer[1]
+
     spread_out(
         0,
-        PLANE,
         in_plane,
-        lambda k: part_y.at[lax.rem(here + k, PLANE)],
+        lambda peer: part_y.at[place_in_plane(peer)],
         lambda k: recv_y.at[k - 1],
     )
-    apply_element(image, get, 0, local2, 0)
+    apply_to_image(0)
     wait_bytes(recv_y, red_recv.at[0])
     total = part_y[here]
     for k in range(PLANE - 1):
         total += recv_y[k]
     sum_b[...] = total
-    spread_out(1, RING, in_ring, lambda k: sum_b, lambda k: recv_b.at[k - 1])
-    apply_element(image, get, 1, local2, 1)
+    spread_out(1, in_ring, lambda peer: sum_b, lambda k: recv_b.at[k - 1])
+    apply_to_image(1)
     wait_bytes(recv_b, red_recv.at[1])
     total = sum_b[...]
     for k in range(RING - 1):
         total += recv_b[k]
     all_y[here] = total
-    spread_out(2, PLANE, in_plane, lambda k: all_y.at[here], lambda k: all_y.at[here])
-    apply_element(image, get, 2, local2, 0)
+    spread_out(2, in_plane, lambda peer: all_y.at[here], lambda k: all_y.at[here])
+    apply_to_image(2)
     wait_bytes(all_y.at[pl.ds(0, PLANE - 1)], red_recv.at[2])
 
     sums = [jnp.zeros((32, 256), F32) for _ in range(3)]
@@ -417,8 +476,29 @@
             probe[m, rows_of(p), :] = get(image, m, rows_of(p)) + cblock[m]
     probe_out = pltpu.make_async_copy(probe, probe_hbm, out_sem.at[0])
     probe_out.start()
+    assemble_inside(local2, second)
+
+    def weighed(value, weights):
+        return jnp.sum(jnp.sum(value * weights, axis=0, keepdims=True), axis=1, keepdims=True)
+
+    row32 = lax.broadcasted_iota(jnp.int32, (32, 1), 0) % 8
+    inner = jnp.where((row32 == 0) | (row32 == 7), 0.0, plane[1])
+    acc_in_sp, acc_in_pp, acc_pp = (jnp.zeros((32, 256), F32) for _ in range(3))
+    for p in range(8):
+        pp = jnp.zeros((32, 256), F32)
+        for m in range(3):
+            pr = probe[m, rows_of(p), :]
+            pp += pr * pr
+            if 0 < p < 7:
+                acc_in_sp += get(second, m, rows_of(p)) * pr
+        if 0 < p < 7:
+            acc_in_pp += pp
+        acc_pp += (0.5 if p in (0, 7) else 1.0) * pp
+    in_sp, in_pp, pp = weighed(acc_in_sp, inner), weighed(acc_in_pp, inner), weighed(acc_pp, plane[1])
+    own = jnp.where(in_pp > 0, in_sp / jnp.where(in_pp > 0, in_pp, 1.0), 0.0)
+
     wait_halo(1, halo_recv)
-    assemble(1, local2, second)
+    assemble_faces(1, local2, second)
     second_out = [
         pltpu.make_async_copy(
             second.at[:, h], sec_hbm.at[:, :, pl.ds(128 * h, 128)], out_sem.at[1 + h]
@@ -427,25 +507,6 @@
     ]
     for out in second_out:
         out.start()
-
-    def both_sums(one, two):
-        results = []
-        for value in (one, two):
-            results.append(jnp.sum(jnp.sum(value * plane[1], axis=0, keepdims=True), axis=1, keepdims=True))
-        return results
-
-    acc_sp, acc_pp = jnp.zeros((32, 256), F32), jnp.zeros((32, 256), F32)
-    for p in range(8):
-        sp, pp = jnp.zeros((32, 256), F32), jnp.zeros((32, 256), F32)
-        for m in range(3):
-            pr = probe[m, rows_of(p), :]
-            sp += get(second, m, rows_of(p)) * pr
-            pp += pr * pr
-        scale = 0.5 if p in (0, 7) else 1.0
-        acc_sp += scale * sp
-        acc_pp += scale * pp
-    sp, pp = both_sums(acc_sp, acc_pp)
-    own = jnp.where(pp > 0, sp / jnp.where(pp > 0, pp, 1.0), 0.0)
     acc_q, acc_rr = jnp.zeros((32, 256), F32), jnp.zeros((32, 256), F32)
     for p in range(8):
         q, rr = jnp.zeros((32, 256), F32), jnp.zeros((32, 256), F32)
@@ -457,37 +518,23 @@
         scale = 0.5 if p in (0, 7) else 1.0
         acc_q += scale * q
         acc_rr += scale * rr
-    q, rr = both_sums(acc_q, acc_rr)
+    q, rr = weighed(acc_q, plane[1]), weighed(acc_rr, plane[1])
 
     lane128 = lax.broadcasted_iota(jnp.int32, (1, 128), 1)
-
-    def pack(one, two, three, four):
-        rest = jnp.where(lane128 < 96, three, four)
-        return jnp.where(lane128 < 32, one, jnp.where(lane128 < 64, two, rest))
-
-    def unpack(rows):
-        return rows, pltpu.roll(rows, 96, 1), pltpu.roll(rows, 64, 1), pltpu.roll(rows, 32, 1)
 
     def total_of(rows):
         return jnp.sum(rows, axis=0, keepdims=True)
 
-    def gather_rows(own_row, ref, count):
-        return jnp.concatenate([own_row] + [ref[k] for k in range(count)], axis=0)
-
-    message = pack(own, q, pp, rr)
-    row_a[...] = message
-    spread_out(3, PLANE, in_plane, lambda k: row_a, lambda k: recv_ra.at[k - 1])
-    wait_bytes(recv_ra, red_recv.at[3])
-    own, q, pp, rr = unpack(gather_rows(message, recv_ra, PLANE - 1))
-    mean_sp, mean_pp = total_of(q + own * pp), total_of(pp)
-    merged = jnp.where(mean_pp > 0, mean_sp / jnp.where(mean_pp > 0, mean_pp, 1.0), 0.0)
-    away = own - merged
-    q, rr = total_of(q + away * pp), total_of(rr + 2.0 * away * q + away * away * pp)
-    message = pack(merged, pltpu.roll(q, 32, 1), pltpu.roll(mean_pp, 64, 1), pltpu.roll(rr, 96, 1))
-    row_b[...] = message
-    spread_out(4, RING, in_ring, lambda k: row_b, lambda k: recv_rb.at[k - 1])
-    wait_bytes(recv_rb, red_recv.at[4])
-    own, q, pp, rr = unpack(gather_rows(message, recv_rb, RING - 1))
+    row_a[...] = jnp.where(
+        lane128 < 32,
+        own,
+        jnp.where(lane128 < 64, q, jnp.where(lane128 < 96, pp, rr)),
+    )
+    spread_out(3, everyone, lambda peer: row_a, lambda k: recv_ra.at[pl.ds(k - 1, 1), :])
+    recv_ra[pl.ds(255, 1), :] = row_a[...]
+    wait_bytes(recv_ra.at[pl.ds(0, 255)], red_recv.at[3])
+    own = recv_ra[...]
+    q, pp, rr = (pltpu.roll(own, shift, 1) for shift in (96, 64, 32))
     weight_total = 343.0 * 128 * slabs * columns
     mean_sp, mean_pp = total_of(q + own * pp) / weight_total, total_of(pp) / weight_total
     coef = mean_sp / (mean_pp + epsilon)
@@ -501,11 +548,43 @@
     wait_bytes(recv_y, red_send.at[0])
     wait_bytes(recv_b, red_send.at[1])
     wait_bytes(all_y.at[pl.ds(0, PLANE - 1)], red_send.at[2])
-    wait_bytes(recv_ra, red_send.at[3])
-    wait_bytes(recv_rb, red_send.at[4])
+    wait_bytes(recv_ra.at[pl.ds(0, 255)], red_send.at[3])
     probe_out.wait()
     for out in second_out:
         out.wait()
+
+
+def normalise(second_hbm, probe_hbm, scal_hbm, basis_hbm, hess, second, probe, scal, basis, sems):
+    parts = [(m, pl.ds(128 * h, 128)) for m in range(3) for h in range(2)]
+    scalars = pltpu.make_async_copy(scal_hbm, scal, sems.at[18])
+    scalars.start()
+    loads = []
+    for i, (m, rows) in enumerate(parts):
+        loads.append(
+            [
+                pltpu.make_async_copy(src.at[m, rows], dst.at[m, rows], sems.at[i + n])
+                for src, dst, n in ((second_hbm, second, 0), (probe_hbm, probe, 6))
+            ]
+        )
+        for load in loads[-1]:
+            load.start()
+    scalars.wait()
+    coef, scale = scal[0:1, 0:1], scal[2:3, 0:1]
+    hess[0] = scal[0, 0]
+    hess[1] = scal[1, 0]
+    stores = []
+    for i, (m, rows) in enumerate(parts):
+        for load in loads[i]:
+            load.wait()
+        for p in range(4):
+            at = pl.ds(rows.start + 32 * p, 32)
+            basis[m, at, :] = (second[m, at, :] - coef * probe[m, at, :]) * scale
+        stores.append(
+            pltpu.make_async_copy(basis.at[m, rows], basis_hbm.at[m, rows], sems.at[12 + i])
+        )
+        stores[-1].start()
+    for store in stores:
+        store.wait()
 
 
 def shards(slabs, columns, state, direction, xxt_rows, coarse_ids):
@@ -526,7 +605,7 @@
             jax.ShapeDtypeStruct(field, F32),
             jax.ShapeDtypeStruct((8, 128), F32),
         ),
-        in_specs=[anywhere] * 7,
+        in_specs=[pl.BlockSpec(memory_space=pltpu.HBM)] * 7,
         out_specs=(anywhere, anywhere, pl.BlockSpec(memory_space=vmem)),
         scratch_shapes=[
             vmem(field, F32),
@@ -536,9 +615,11 @@
             vmem((768, 512), BF16),
             vmem((512, 512), BF16),
             vmem((2, 32, 256), F32),
+            vmem((2,) + field, BF16),
+            vmem((2,) + field, BF16),
             vmem((3, 3, 256, 256), F32),
-            vmem((2, 768, 256), F32),
-            vmem((2, 256, 512), F32),
+            vmem((3, 768, 256), F32),
+            vmem((3, 256, 512), F32),
             vmem(halved, F32),
             vmem(halved, F32),
             vmem(halved, F32),
@@ -560,18 +641,16 @@
             vmem((2, 3, 8, 256), F32),
             vmem((2, 4, 4, 256), F32),
             vmem((1, 128), F32),
-            vmem((PLANE - 1, 1, 128), F32),
-            vmem((1, 128), F32),
-            vmem((RING - 1, 1, 128), F32),
-            pltpu.SemaphoreType.DMA((7,)),
+            vmem((256, 128), F32),
+            pltpu.SemaphoreType.DMA((11,)),
             pltpu.SemaphoreType.DMA((3,)),
             pltpu.SemaphoreType.DMA((2, 8)),
             pltpu.SemaphoreType.DMA((2, 8)),
-            pltpu.SemaphoreType.DMA((5,)),
-            pltpu.SemaphoreType.DMA((5,)),
+            pltpu.SemaphoreType.DMA((4,)),
+            pltpu.SemaphoreType.DMA((4,)),
         ],
         compiler_params=pltpu.CompilerParams(
-            collective_id=0, has_side_effects=True, vmem_limit_bytes=40 * 1024 * 1024
+            collective_id=0, has_side_effects=True, vmem_limit_bytes=VMEM_LIMIT
         ),
         name="jacobian_products",
     )(
@@ -583,8 +662,25 @@
         jnp.asarray(right),
         jnp.asarray(plane),
     )
-    next_basis = (sec - scal[0, 0] * probe) * scal[2, 0]
-    return next_basis.reshape(shape), scal[:2, 0]
+    next_basis, hessenberg = pl.pallas_call(
+        normalise,
+        out_shape=(jax.ShapeDtypeStruct(field, F32), jax.ShapeDtypeStruct((2,), F32)),
+        in_specs=[pl.BlockSpec(memory_space=pltpu.HBM)] * 3,
+        out_specs=(
+            pl.BlockSpec(memory_space=pltpu.HBM),
+            pl.BlockSpec(memory_space=pltpu.SMEM),
+        ),
+        scratch_shapes=[
+            vmem(field, F32),
+            vmem(field, F32),
+            vmem((8, 128), F32),
+            vmem(field, F32),
+            pltpu.SemaphoreType.DMA((19,)),
+        ],
+        compiler_params=pltpu.CompilerParams(vmem_limit_bytes=VMEM_LIMIT),
+        name="normalise",
+    )(sec, probe, scal)
+    return next_basis.reshape(shape), hessenberg
 
 
 def solution(mesh):

time: 61.2 us -> 52.3 us (0.85)
  local copies, waits for them, and re-layouts: 8.37 us -> 0 us
  other arithmetic: 2.23 us -> 0 us
  Pallas kernels: 49.6 us -> 51.5 us
    unnamed x14 -> x0, local copies, waits for them, and re-layouts: 7.15 us -> none
    pallas_call x0 -> x1, Pallas kernels: none -> 2.8 us  [shards(): pl.pallas_call(normalise, out_shape=(jax.ShapeDtypeStruct(field, F32), ja...]
    mul x1 -> x0, other arithmetic: 2.23 us -> none  [shards(): next_basis = (sec - scal[0, 0] * probe) * scal[2, 0]]
    slice x2 -> x0, local copies, waits for them, and re-layouts: 1.22 us -> none  [the longest x1 0.63 us: shards(): return (next_basis.reshape(shape), scal[:2, 0])]
    pallas_call x1, Pallas kernels: 49.6 us -> 48.7 us  [shards(): pl.pallas_call(body, out_shape=(jax.ShapeDtypeStruct(field, F32), jax.Sha...]
where the time goes in v2:
time: 52.3 us; the launch traced here: 52.1 us
  Pallas kernels  51.5 us (98%)
  between operations  0.64 us (1%)
    pallas_call x1, Pallas kernels, shards(): pl.pallas_call(body, out_shape=(jax.ShapeDtypeStruct(field, F32), jax.Sha...  48.7 us
    pallas_call x1, Pallas kernels, shards(): pl.pallas_call(normalise, out_shape=(jax.ShapeDtypeStruct(field, F32), ja...  2.8 us

profile of v2, /device:TPU:1, one launch (start us, length us, event | category | flops | bytes accessed | tf_op | source)
XLA Modules:
  0.0 52.1 jit_solution(16633839913877140030)
XLA Ops:
  0.6 48.7 %jacobian_products.1 = (f32[3,256,256]{2,1,0:T(8,128)}, f32[3,256,256]{2,1,0:T(8,128)}, f32[8,128]{1,0:T(8,128)}) custom-call(f32[3,256,256]{2,1,0:T(8,128)} %bitcast.3, f32[3,256,256]{2,1,0:T(8,128)} %bitcast.4, f32[32,8192]{1,0:T(8,128)} %refs_2_.1, s32[1,128]{1,0:T(1,128)} %refs_3_.1, bf16[768,512]{1,0:T(8,128)(2,1)} %constant.6.clone.refs_4_, ...), custom_call_target="tpu_custom_call" | custom-call | tf_op jit(solution)/shard_map/jacobian_products/pallas_call | solution.py:601
  49.3 2.8 %normalise.1 = (f32[3,256,256]{2,1,0:T(8,128)}, f32[2]{0:T(128)}) custom-call(f32[3,256,256]{2,1,0:T(8,128)} %get-tuple-element.7.second_hbm, f32[3,256,256]{2,1,0:T(8,128)} %get-tuple-element.8.probe_hbm, f32[8,128]{1,0:T(8,128)} %get-tuple-element.9.scal_hbm), custom_call_target="tpu_custom_call" | custom-call | tf_op jit(solution)/shard_map/normalise/pallas_call | solution.py:665

commit v3 on v2

--- a/solution.py
+++ b/solution.py
@@ -89,13 +89,10 @@
         for plane in planes
     ]
     left = np.concatenate(left, axis=0)
-    right = np.concatenate([np.kron(eye(32), derivative.T), np.kron(eye(32), stiff.T)], axis=1)
+    right = np.concatenate([np.kron(eye(16), derivative.T), np.kron(eye(16), stiff.T)], axis=1)
     left = np.concatenate(halves(left), axis=1)
     right = np.concatenate(halves(right), axis=0)
-    half = np.where((np.arange(8) == 0) | (np.arange(8) == 7), 0.5, 1.0)
-    mass = np.tile(weights, 4)[:, None] * np.tile(weights, 32)[None, :]
-    count = np.tile(half, 4)[:, None] * np.tile(half, 32)[None, :]
-    return left, right, np.stack([mass, count]).astype(np.float32), weights
+    return left, right
 
 
 WEIGHTS = tables()[1]
@@ -115,7 +112,6 @@
     ids_hbm,
     left_hbm,
     right_hbm,
-    plane_hbm,
     sec_hbm,
     probe_hbm,
     scal_ref,
@@ -136,6 +132,8 @@
     local2,
     second,
     probe,
+    ysides,
+    tsum,
     onehot,
     cblock,
     part_y,
@@ -176,10 +174,12 @@
     def beside(dx, dy):
         return (lax.rem(gx + dx + slabs, slabs), lax.rem(yz + dy + columns, columns))
 
-    pairs = [(left_hbm, left), (state_hbm.at[0], state.at[0]), (right_hbm, right)]
-    pairs += [(state_hbm.at[m], state.at[m]) for m in (1, 2)]
+    faces, inside_rows = pl.ds(0, 192), pl.ds(192, 576)
+    pairs = [(left_hbm.at[faces], left.at[faces]), (right_hbm, right)]
+    pairs += [(state_hbm.at[m], state.at[m]) for m in range(3)]
     pairs += [(dir_hbm.at[m], direc.at[m]) for m in range(3)]
-    pairs += [(plane_hbm, plane), (ids_hbm, ids), (xxt_hbm, xxt)]
+    pairs += [(left_hbm.at[inside_rows], left.at[inside_rows])]
+    pairs += [(ids_hbm, ids), (xxt_hbm, xxt)]
     loads = [pltpu.make_async_copy(src, dst, in_sem.at[i]) for i, (src, dst) in enumerate(pairs)]
     for load in loads[:-1]:
         load.start()
@@ -194,6 +194,20 @@
     from_next = ((lane % 8 == 7) & (lane != 255)).astype(F32)
     from_last = ((lane % 8 == 0) & (lane != 0)).astype(F32)
     inside = ((lane != 0) & (lane != 255)).astype(F32)
+
+    def by_place(place, values):
+        place = place % 8
+        place = jnp.minimum(place, 7 - place)
+        result = jnp.full(place.shape, values[0], F32)
+        for i in range(1, 4):
+            result = jnp.where(place == i, float(values[i]), result)
+        return result
+
+    row32 = lax.broadcasted_iota(jnp.int32, (32, 1), 0)
+    half = (0.5, 1.0, 1.0, 1.0)
+    weights4 = [float(w) for w in WEIGHTS[:4]]
+    plane[0] = by_place(row32, weights4) * by_place(lane, weights4)
+    plane[1] = by_place(row32, half) * by_place(lane, half)
     wall_xl = jnp.where(gx == 0, 0.0, 1.0).astype(F32)
     wall_xh = jnp.where(gx == slabs - 1, 0.0, 1.0).astype(F32)
     wall_yl = jnp.where(yz == 0, 0.0, 1.0).astype(F32)
@@ -238,20 +252,23 @@
 
     def products_right(which, m, g, cols):
         ops = right[:, pl.ds(0, cols)]
-        high, low = (
-            jnp.concatenate([ref[which, m, rows_of(p), :] for p in GROUPS[g][2]], axis=0)
-            for ref in (highs, lows)
-        )
-        return jnp.dot(
-            jnp.concatenate([high, high, low], axis=1),
-            jnp.concatenate([ops, ops[:256]], axis=0),
-            preferred_element_type=F32,
-        )
+        ops = jnp.concatenate([ops, ops[:128]], axis=0)
+        results = []
+        for h in range(2):
+            high, low = (
+                jnp.concatenate(
+                    [ref[which, m, rows_of(p), pl.ds(128 * h, 128)] for p in GROUPS[g][2]], axis=0
+                )
+                for ref in (highs, lows)
+            )
+            both = jnp.concatenate([high, high, low], axis=1)
+            results.append(jnp.dot(both, ops, preferred_element_type=F32))
+        return results
 
     def state_gradients(m, g):
         _, size, planes = GROUPS[g]
         by_left = products_left(0, m, g, 2)
-        by_right = products_right(0, m, g, 256)
+        by_right = jnp.concatenate(products_right(0, m, g, 128), axis=1)
         for i, p in enumerate(planes):
             grads[m, 0, rows_of(p), :] = by_left[32 * i : 32 * i + 32]
             grads[m, 1, rows_of(p), :] = by_left[size + 32 * i : size + 32 * i + 32]
@@ -260,19 +277,23 @@
     def multiply(which, m, g):
         first, size, planes = GROUPS[g]
         lhs_out[m, pl.ds(first, 3 * size), :] = products_left(which, m, g, 3)
-        by_right = products_right(which, m, g, 512)
-        for i, p in enumerate(planes):
-            rhs_out[m, rows_of(p), :] = by_right[32 * i : 32 * i + 32]
+        for h, by_right in enumerate(products_right(which, m, g, 256)):
+            for i, p in enumerate(planes):
+                rhs_out[m, h, rows_of(p), :] = by_right[32 * i : 32 * i + 32]
+
+    def along_z(m, rows, kind):
+        part = pl.ds(128 * kind, 128)
+        return jnp.concatenate([rhs_out[m, 0, rows, part], rhs_out[m, 1, rows, part]], axis=1)
 
     def combine(vector, take, m, g, target):
         first, size, planes = GROUPS[g]
         for i, p in enumerate(planes):
             rows = rows_of(p)
             at = [pl.ds(first + size * op + 32 * i, 32) for op in range(3)]
-            total = lhs_out[m, at[2], :] + rhs_out[m, rows, pl.ds(256, 256)]
+            total = lhs_out[m, at[2], :] + along_z(m, rows, 1)
             total += state[0, rows, :] * lhs_out[m, at[0], :]
             total += state[1, rows, :] * lhs_out[m, at[1], :]
-            total += state[2, rows, :] * rhs_out[m, rows, pl.ds(0, 256)]
+            total += state[2, rows, :] * along_z(m, rows, 0)
             for k in range(3):
                 total += take(vector, k, rows) * grads[m, k, rows, :]
             put(target, m, rows, total * (plane[0] * float(WEIGHTS[p])))
@@ -297,20 +318,18 @@
         send(turn, 0, source.at[m, :, pl.ds(224, 32), :], recv_xl.at[turn, m], beside(1, 0))
         send(turn, 1, source.at[m, :, pl.ds(0, 32), :], recv_xh.at[turn, m], beside(-1, 0))
 
-    def send_y(turn, source):
+    def send_corners(turn, source):
         for m in range(3):
-            low = get(source, m, pl.ds(0, 8, stride=32))
-            high = get(source, m, pl.ds(31, 8, stride=32))
-            send_yl[turn, m] = low
-            send_yh[turn, m] = high
-            send_c[turn, 0, pl.ds(m, 1), :] = low[0:1]
-            send_c[turn, 1, pl.ds(m, 1), :] = high[0:1]
-            send_c[turn, 2, pl.ds(m, 1), :] = low[7:8]
-            send_c[turn, 3, pl.ds(m, 1), :] = high[7:8]
-        send(turn, 2, send_yh.at[turn], recv_yl.at[turn], beside(0, 1))
-        send(turn, 3, send_yl.at[turn], recv_yh.at[turn], beside(0, -1))
+            for i, row in enumerate((0, 31, 224, 255)):
+                send_c[turn, i, pl.ds(m, 1), :] = get(source, m, pl.ds(row, 1))
         for i, (dx, dy) in enumerate(((-1, -1), (-1, 1), (1, -1), (1, 1))):
             send(turn, 4 + i, send_c.at[turn, i], recv_c.at[turn, i], beside(dx, dy))
+
+    def send_y(turn, source, m):
+        send_yl[turn, m] = get(source, m, pl.ds(0, 8, stride=32))
+        send_yh[turn, m] = get(source, m, pl.ds(31, 8, stride=32))
+        send(turn, 2, send_yh.at[turn, m], recv_yl.at[turn, m], beside(0, 1))
+        send(turn, 3, send_yl.at[turn, m], recv_yh.at[turn, m], beside(0, -1))
 
     def halo_refs(turn):
         refs = [recv_xl.at[turn], recv_xh.at[turn], recv_yl.at[turn], recv_yh.at[turn]]
@@ -320,12 +339,16 @@
         for i, ref in enumerate(halo_refs(turn)):
             pltpu.make_async_copy(ref, ref, sems.at[turn, i]).wait()
 
-    def assemble_inside(source, target):
+    def fold_y(target, first, count, stride):
         for m in range(3):
-            for p in range(1, 7):
-                put(target, m, rows_of(p), fold_z(get(source, m, rows_of(p))))
-
-    def assemble_faces(turn, source, target):
+            for b in range(3):
+                one = pl.ds(first + 8 * b + 7, count, stride=stride)
+                two = pl.ds(first + 8 * b + 8, count, stride=stride)
+                both = get(target, m, one) + get(target, m, two)
+                put(target, m, one, both)
+                put(target, m, two, both)
+
+    def assemble_planes(turn, source, target):
         for m in range(3):
             value = get(source, m, rows_of(0)) + get(recv_xl.at[turn], m, pl.ds(0, 32))
             put(target, m, rows_of(0), fold_z(value * wall_xl))
@@ -338,14 +361,14 @@
             high = recv_yh[turn, m]
             high += jnp.where(row8 == 0, recv_c[turn, 2, at_m, :], 0.0)
             high += jnp.where(row8 == 7, recv_c[turn, 0, at_m, :], 0.0)
-            first, last = pl.ds(0, 8, stride=32), pl.ds(31, 8, stride=32)
-            put(target, m, first, (get(target, m, first) + fold_z(low) * wall_x) * wall_yl)
-            put(target, m, last, (get(target, m, last) + fold_z(high) * wall_x) * wall_yh)
-            for b in range(3):
-                one, two = pl.ds(8 * b + 7, 8, stride=32), pl.ds(8 * b + 8, 8, stride=32)
-                both = get(target, m, one) + get(target, m, two)
-                put(target, m, one, both)
-                put(target, m, two, both)
+            ysides[0, m] = fold_z(low) * wall_x
+            ysides[1, m] = fold_z(high) * wall_x
+
+    def assemble_sides(target):
+        first, last = pl.ds(0, 8, stride=32), pl.ds(31, 8, stride=32)
+        for m in range(3):
+            put(target, m, first, (get(target, m, first) + ysides[0, m]) * wall_yl)
+            put(target, m, last, (get(target, m, last) + ysides[1, m]) * wall_yh)
 
     def spread_out(phase, places, src_of, dst_of):
         for k, place in places:
@@ -363,29 +386,36 @@
         pltpu.make_async_copy(ref, ref, sem).wait()
 
     loads[0].wait()
-    for m in range(3):
-        loads[(1, 3, 4)[m]].wait()
+    loads[1].wait()
+    for m in range(3):
+        loads[2 + m].wait()
         split_into(state[m], 0, m)
-        if m == 0:
-            loads[2].wait()
         state_gradients(m, 0)
     for m in range(3):
         loads[5 + m].wait()
         split_into(direc[m], 1, m)
+    for m in range(3):
         multiply(1, m, 0)
-    loads[8].wait()
-    for m in range(3):
         combine(direc, whole, m, 0, local)
         if m == 0:
             pl.semaphore_wait(barrier, len(greeted))
         send_x(0, local, m)
+    send_corners(0, local)
     loads[10].start()
+    loads[8].wait()
     for m in range(3):
         state_gradients(m, 1)
         multiply(1, m, 1)
         combine(direc, whole, m, 1, local)
-    send_y(0, local)
-    assemble_inside(local, image)
+        send_y(0, local, m)
+    for m in range(3):
+        total = jnp.zeros((32, 256), F32)
+        for p in range(1, 7):
+            value = fold_z(get(local, m, rows_of(p)))
+            put(image, m, rows_of(p), value)
+            total += float(WEIGHTS[p]) * value
+        tsum[m] = total
+    fold_y(image, 32, 6, 32)
 
     loads[9].wait()
     elem = lax.broadcasted_iota(jnp.int32, (128, 1024), 0)
@@ -401,36 +431,42 @@
     loads[10].wait()
 
     wait_halo(0, halo_recv)
-    assemble_faces(0, local, image)
-
+    assemble_planes(0, local, image)
+
+    weight8 = by_place(row8, weights4)
+    y_next = ((row32 % 8 == 7) & (row32 != 31)).astype(F32)
+    y_last = ((row32 % 8 == 0) & (row32 != 0)).astype(F32)
+    wall_y = jnp.where(row32 == 0, wall_yl, jnp.where(row32 == 31, wall_yh, 1.0))
     coarse = []
     for m in range(3):
-        total = get(image, m, rows_of(0)) * float(WEIGHTS[0])
-        for p in range(1, 8):
-            total += get(image, m, rows_of(p)) * float(WEIGHTS[p])
-        total *= plane[0]
+        total = tsum[m] + float(WEIGHTS[0]) * (get(image, m, rows_of(0)) + get(image, m, rows_of(7)))
+        low, high = (
+            jnp.sum(ysides[i, m] * weight8, axis=0, keepdims=True) for i in range(2)
+        )
+        total += jnp.where(row32 == 0, low, 0.0) + jnp.where(row32 == 31, high, 0.0)
+        folded = total + pltpu.roll(total, 31, 0) * y_next + pltpu.roll(total, 1, 0) * y_last
+        folded *= plane[0] * wall_y
         acc = jnp.zeros((32, 256), F32)
         for b in range(4):
-            line = jnp.sum(total[8 * b : 8 * b + 8], axis=0, keepdims=True)
+            line = jnp.sum(folded[8 * b : 8 * b + 8], axis=0, keepdims=True)
             acc += onehot[:, pl.ds(256 * b, 256)] * line
         coarse.append(jnp.sum(acc, axis=1, keepdims=True))
-    for j in range(PLANE):
-        block = xxt[:, pl.ds(256 * j, 256)]
+
+    def form_part(slot, peer):
+        chunk = lax.rem(peer[0], 4) * columns + peer[1]
+        block = xxt[:, pl.ds(pl.multiple_of(chunk * 256, 256), 256)]
         for m in range(3):
-            part_y[j, pl.ds(m, 1), :] = jnp.sum(block * coarse[m], axis=0, keepdims=True)
-
-    def place_in_plane(peer):
-        return lax.rem(peer[0], 4) * columns + peer[1]
-
-    spread_out(
-        0,
-        in_plane,
-        lambda peer: part_y.at[place_in_plane(peer)],
-        lambda k: recv_y.at[k - 1],
-    )
+            part_y[slot, pl.ds(m, 1), :] = jnp.sum(block * coarse[m], axis=0, keepdims=True)
+
+    for k, place in in_plane:
+        form_part(k, peer_at(place))
+        spread_out(0, [(k, place)], lambda peer: part_y.at[k], lambda k: recv_y.at[k - 1])
+    form_part(0, (gx, yz))
+    assemble_sides(image)
+    fold_y(image, 0, 2, 224)
     apply_to_image(0)
     wait_bytes(recv_y, red_recv.at[0])
-    total = part_y[here]
+    total = part_y[0]
     for k in range(PLANE - 1):
         total += recv_y[k]
     sum_b[...] = total
@@ -467,58 +503,83 @@
         add_correction(m, 0)
         add_correction(m, 7)
         send_x(1, local2, m)
+    send_corners(1, local2)
     for m in range(3):
         for p in range(1, 7):
             add_correction(m, p)
-    send_y(1, local2)
+        send_y(1, local2, m)
     for m in range(3):
         for p in range(8):
-            probe[m, rows_of(p), :] = get(image, m, rows_of(p)) + cblock[m]
-    probe_out = pltpu.make_async_copy(probe, probe_hbm, out_sem.at[0])
-    probe_out.start()
-    assemble_inside(local2, second)
+            put(probe, m, rows_of(p), get(image, m, rows_of(p)) + cblock[m])
+
+    def copies_out(source, target, n):
+        copies = [
+            pltpu.make_async_copy(
+                source.at[:, h], target.at[:, :, pl.ds(128 * h, 128)], out_sem.at[n + h]
+            )
+            for h in range(2)
+        ]
+        for copy in copies:
+            copy.start()
+        return copies
+
+    outs = copies_out(probe, probe_hbm, 0)
+    for m in range(3):
+        for p in range(1, 7):
+            put(second, m, rows_of(p), fold_z(get(local2, m, rows_of(p))))
 
     def weighed(value, weights):
         return jnp.sum(jnp.sum(value * weights, axis=0, keepdims=True), axis=1, keepdims=True)
 
-    row32 = lax.broadcasted_iota(jnp.int32, (32, 1), 0) % 8
-    inner = jnp.where((row32 == 0) | (row32 == 7), 0.0, plane[1])
+    inner = jnp.where((row32 % 8 == 0) | (row32 % 8 == 7), 0.0, plane[1])
     acc_in_sp, acc_in_pp, acc_pp = (jnp.zeros((32, 256), F32) for _ in range(3))
     for p in range(8):
         pp = jnp.zeros((32, 256), F32)
         for m in range(3):
-            pr = probe[m, rows_of(p), :]
+            pr = get(probe, m, rows_of(p))
             pp += pr * pr
             if 0 < p < 7:
                 acc_in_sp += get(second, m, rows_of(p)) * pr
         if 0 < p < 7:
             acc_in_pp += pp
         acc_pp += (0.5 if p in (0, 7) else 1.0) * pp
-    in_sp, in_pp, pp = weighed(acc_in_sp, inner), weighed(acc_in_pp, inner), weighed(acc_pp, plane[1])
+    in_sp, in_pp, pp = (
+        weighed(acc_in_sp, inner),
+        weighed(acc_in_pp, inner),
+        weighed(acc_pp, plane[1]),
+    )
     own = jnp.where(in_pp > 0, in_sp / jnp.where(in_pp > 0, in_pp, 1.0), 0.0)
+    fold_y(second, 32, 6, 32)
+
+    def residual_sums(places):
+        q, rr = 0.0, 0.0
+        for rows in places:
+            for m in range(3):
+                pr = get(probe, m, rows)
+                rest = get(second, m, rows) - own * pr
+                q += rest * pr
+                rr += rest * rest
+        return q, rr
+
+    not_sides = jnp.where((row32 == 0) | (row32 == 31), 0.0, plane[1])
+    sums_in = [v * not_sides for v in residual_sums([rows_of(p) for p in range(1, 7)])]
 
     wait_halo(1, halo_recv)
-    assemble_faces(1, local2, second)
-    second_out = [
-        pltpu.make_async_copy(
-            second.at[:, h], sec_hbm.at[:, :, pl.ds(128 * h, 128)], out_sem.at[1 + h]
+    assemble_planes(1, local2, second)
+    assemble_sides(second)
+    fold_y(second, 0, 2, 224)
+    outs += copies_out(second, sec_hbm, 2)
+    sums_faces = residual_sums([rows_of(0), rows_of(7)])
+    sums_sides = residual_sums([pl.ds(32, 6, stride=32), pl.ds(63, 6, stride=32)])
+    q, rr = (
+        jnp.sum(
+            jnp.sum(one + two * (0.5 * plane[1]), axis=0, keepdims=True)
+            + jnp.sum(three, axis=0, keepdims=True) * plane[1, 0:1, :],
+            axis=1,
+            keepdims=True,
         )
-        for h in range(2)
-    ]
-    for out in second_out:
-        out.start()
-    acc_q, acc_rr = jnp.zeros((32, 256), F32), jnp.zeros((32, 256), F32)
-    for p in range(8):
-        q, rr = jnp.zeros((32, 256), F32), jnp.zeros((32, 256), F32)
-        for m in range(3):
-            pr = probe[m, rows_of(p), :]
-            rest = get(second, m, rows_of(p)) - own * pr
-            q += rest * pr
-            rr += rest * rest
-        scale = 0.5 if p in (0, 7) else 1.0
-        acc_q += scale * q
-        acc_rr += scale * rr
-    q, rr = weighed(acc_q, plane[1]), weighed(acc_rr, plane[1])
+        for one, two, three in zip(sums_in, sums_faces, sums_sides)
+    )
 
     lane128 = lax.broadcasted_iota(jnp.int32, (1, 128), 1)
 
@@ -549,8 +610,7 @@
     wait_bytes(recv_b, red_send.at[1])
     wait_bytes(all_y.at[pl.ds(0, PLANE - 1)], red_send.at[2])
     wait_bytes(recv_ra.at[pl.ds(0, 255)], red_send.at[3])
-    probe_out.wait()
-    for out in second_out:
+    for out in outs:
         out.wait()
 
 
@@ -589,7 +649,7 @@
 
 def shards(slabs, columns, state, direction, xxt_rows, coarse_ids):
     shape = state.shape
-    left, right, plane, _ = constants()
+    left, right = constants()
     vmem = pltpu.VMEM
     field = (3, 256, 256)
     halved = (3, 2, 256, 128)
@@ -605,7 +665,7 @@
             jax.ShapeDtypeStruct(field, F32),
             jax.ShapeDtypeStruct((8, 128), F32),
         ),
-        in_specs=[pl.BlockSpec(memory_space=pltpu.HBM)] * 7,
+        in_specs=[pl.BlockSpec(memory_space=pltpu.HBM)] * 6,
         out_specs=(anywhere, anywhere, pl.BlockSpec(memory_space=vmem)),
         scratch_shapes=[
             vmem(field, F32),
@@ -613,18 +673,20 @@
             vmem((32, 8192), F32),
             vmem((1, 128), jnp.int32),
             vmem((768, 512), BF16),
-            vmem((512, 512), BF16),
+            vmem((256, 256), BF16),
             vmem((2, 32, 256), F32),
             vmem((2,) + field, BF16),
             vmem((2,) + field, BF16),
             vmem((3, 3, 256, 256), F32),
             vmem((3, 768, 256), F32),
-            vmem((3, 256, 512), F32),
+            vmem((3, 2, 256, 256), F32),
             vmem(halved, F32),
             vmem(halved, F32),
             vmem(halved, F32),
             vmem(halved, F32),
-            vmem(field, F32),
+            vmem(halved, F32),
+            vmem((2, 3, 8, 256), F32),
+            vmem((3, 32, 256), F32),
             vmem((32, 1024), F32),
             vmem((3, 32, 256), F32),
             vmem((PLANE, 4, 256), F32),
@@ -643,7 +705,7 @@
             vmem((1, 128), F32),
             vmem((256, 128), F32),
             pltpu.SemaphoreType.DMA((11,)),
-            pltpu.SemaphoreType.DMA((3,)),
+            pltpu.SemaphoreType.DMA((4,)),
             pltpu.SemaphoreType.DMA((2, 8)),
             pltpu.SemaphoreType.DMA((2, 8)),
             pltpu.SemaphoreType.DMA((4,)),
@@ -660,7 +722,6 @@
         coarse_ids,
         jnp.asarray(left),
         jnp.asarray(right),
-        jnp.asarray(plane),
     )
     next_basis, hessenberg = pl.pallas_call(
         normalise,

time: 52.3 us -> 50.5 us (0.966)
  Pallas kernels: 51.5 us -> 49.7 us
    pallas_call x1, Pallas kernels: 48.7 us -> 46.9 us  [shards(): pl.pallas_call(body, out_shape=(jax.ShapeDtypeStruct(field, F32), jax.Sha...]
where the time goes in v3:
time: 50.5 us; the launch traced here: 50.3 us
  Pallas kernels  49.7 us (98%)
  between operations  0.64 us (1%)
    pallas_call x1, Pallas kernels, shards(): pl.pallas_call(body, out_shape=(jax.ShapeDtypeStruct(field, F32), jax.Sha...  46.9 us
    pallas_call x1, Pallas kernels, shards(): pl.pallas_call(normalise, out_shape=(jax.ShapeDtypeStruct(field, F32), ja...  2.8 us

profile of v3, /device:TPU:1, one launch (start us, length us, event | category | flops | bytes accessed | tf_op | source)
XLA Modules:
  0.0 50.3 jit_solution(10781984818192035535)
XLA Ops:
  0.6 46.9 %jacobian_products.1 = (f32[3,256,256]{2,1,0:T(8,128)}, f32[3,256,256]{2,1,0:T(8,128)}, f32[8,128]{1,0:T(8,128)}) custom-call(f32[3,256,256]{2,1,0:T(8,128)} %bitcast.3, f32[3,256,256]{2,1,0:T(8,128)} %bitcast.4, f32[32,8192]{1,0:T(8,128)} %refs_2_.1, s32[1,128]{1,0:T(1,128)} %refs_3_.1, bf16[768,512]{1,0:T(8,128)(2,1)} %constant.4.clone.refs_4_, ...), custom_call_target="tpu_custom_call" | custom-call | tf_op jit(solution)/shard_map/jacobian_products/pallas_call | solution.py:661
  47.5 2.8 %normalise.1 = (f32[3,256,256]{2,1,0:T(8,128)}, f32[2]{0:T(128)}) custom-call(f32[3,256,256]{2,1,0:T(8,128)} %get-tuple-element.7.second_hbm, f32[3,256,256]{2,1,0:T(8,128)} %get-tuple-element.8.probe_hbm, f32[8,128]{1,0:T(8,128)} %get-tuple-element.9.scal_hbm), custom_call_target="tpu_custom_call" | custom-call | tf_op jit(solution)/shard_map/normalise/pallas_call | solution.py:726

commit v4 on v3

--- a/solution.py
+++ b/solution.py
@@ -14,7 +14,7 @@
 BF16 = jnp.bfloat16
 PLANE = 32
 RING = 8
-VMEM_LIMIT = 60 * 1024 * 1024
+VMEM_LIMIT = 52 * 1024 * 1024
 
 
 def tables():
@@ -90,9 +90,14 @@
     ]
     left = np.concatenate(left, axis=0)
     right = np.concatenate([np.kron(eye(16), derivative.T), np.kron(eye(16), stiff.T)], axis=1)
-    left = np.concatenate(halves(left), axis=1)
-    right = np.concatenate(halves(right), axis=0)
-    return left, right
+    return np.concatenate(
+        [
+            np.concatenate(halves(left[:192]), axis=1),
+            np.concatenate(halves(right), axis=1),
+            np.concatenate(halves(left[192:]), axis=1),
+        ],
+        axis=0,
+    )
 
 
 WEIGHTS = tables()[1]
@@ -110,8 +115,7 @@
     dir_hbm,
     xxt_hbm,
     ids_hbm,
-    left_hbm,
-    right_hbm,
+    ops_hbm,
     sec_hbm,
     probe_hbm,
     scal_ref,
@@ -119,8 +123,7 @@
     direc,
     xxt,
     ids,
-    left,
-    right,
+    ops_all,
     plane,
     highs,
     lows,
@@ -174,11 +177,11 @@
     def beside(dx, dy):
         return (lax.rem(gx + dx + slabs, slabs), lax.rem(yz + dy + columns, columns))
 
-    faces, inside_rows = pl.ds(0, 192), pl.ds(192, 576)
-    pairs = [(left_hbm.at[faces], left.at[faces]), (right_hbm, right)]
+    first, others = pl.ds(0, 320), pl.ds(320, 576)
+    pairs = [(ops_hbm.at[first], ops_all.at[first])]
     pairs += [(state_hbm.at[m], state.at[m]) for m in range(3)]
     pairs += [(dir_hbm.at[m], direc.at[m]) for m in range(3)]
-    pairs += [(left_hbm.at[inside_rows], left.at[inside_rows])]
+    pairs += [(ops_hbm.at[others], ops_all.at[others])]
     pairs += [(ids_hbm, ids), (xxt_hbm, xxt)]
     loads = [pltpu.make_async_copy(src, dst, in_sem.at[i]) for i, (src, dst) in enumerate(pairs)]
     for load in loads[:-1]:
@@ -242,7 +245,7 @@
 
     def products_left(which, m, g, count):
         first, rows, _ = GROUPS[g]
-        ops = left[pl.ds(first, rows * count), :]
+        ops = ops_all[pl.ds(first + 128 * g, rows * count), :]
         high, low = highs[which, m], lows[which, m]
         return jnp.dot(
             jnp.concatenate([ops, ops[:, :256]], axis=1),
@@ -251,8 +254,9 @@
         )
 
     def products_right(which, m, g, cols):
-        ops = right[:, pl.ds(0, cols)]
-        ops = jnp.concatenate([ops, ops[:128]], axis=0)
+        at = pl.ds(192, 128)
+        high, low = (ops_all[at, pl.ds(start, cols)] for start in (0, 256))
+        ops = jnp.concatenate([high, low, high], axis=0)
         results = []
         for h in range(2):
             high, low = (
@@ -386,13 +390,12 @@
         pltpu.make_async_copy(ref, ref, sem).wait()
 
     loads[0].wait()
-    loads[1].wait()
-    for m in range(3):
-        loads[2 + m].wait()
+    for m in range(3):
+        loads[1 + m].wait()
         split_into(state[m], 0, m)
         state_gradients(m, 0)
     for m in range(3):
-        loads[5 + m].wait()
+        loads[4 + m].wait()
         split_into(direc[m], 1, m)
     for m in range(3):
         multiply(1, m, 0)
@@ -401,8 +404,8 @@
             pl.semaphore_wait(barrier, len(greeted))
         send_x(0, local, m)
     send_corners(0, local)
-    loads[10].start()
-    loads[8].wait()
+    loads[9].start()
+    loads[7].wait()
     for m in range(3):
         state_gradients(m, 1)
         multiply(1, m, 1)
@@ -417,7 +420,7 @@
         tsum[m] = total
     fold_y(image, 32, 6, 32)
 
-    loads[9].wait()
+    loads[8].wait()
     elem = lax.broadcasted_iota(jnp.int32, (128, 1024), 0)
     spot = lax.broadcasted_iota(jnp.int32, (128, 1024), 1)
     wide = jnp.dot(
@@ -428,7 +431,7 @@
     for t in range(4):
         row = (lax.broadcasted_iota(jnp.int32, (8, 1024), 0) + 8 * t).astype(F32)
         onehot[pl.ds(8 * t, 8), :] = jnp.where(jnp.abs(wide - row) < 0.5, 1.0, 0.0)
-    loads[10].wait()
+    loads[9].wait()
 
     wait_halo(0, halo_recv)
     assemble_planes(0, local, image)
@@ -614,33 +617,18 @@
         out.wait()
 
 
-def normalise(second_hbm, probe_hbm, scal_hbm, basis_hbm, hess, second, probe, scal, basis, sems):
-    parts = [(m, pl.ds(128 * h, 128)) for m in range(3) for h in range(2)]
-    scalars = pltpu.make_async_copy(scal_hbm, scal, sems.at[18])
-    scalars.start()
-    loads = []
-    for i, (m, rows) in enumerate(parts):
-        loads.append(
-            [
-                pltpu.make_async_copy(src.at[m, rows], dst.at[m, rows], sems.at[i + n])
-                for src, dst, n in ((second_hbm, second, 0), (probe_hbm, probe, 6))
-            ]
-        )
-        for load in loads[-1]:
-            load.start()
-    scalars.wait()
+def normalise(second, probe, scal, basis_hbm, hess, basis, sems):
     coef, scale = scal[0:1, 0:1], scal[2:3, 0:1]
     hess[0] = scal[0, 0]
     hess[1] = scal[1, 0]
     stores = []
-    for i, (m, rows) in enumerate(parts):
-        for load in loads[i]:
-            load.wait()
+    for i in range(6):
+        m, part = i // 2, pl.ds(128 * (i % 2), 128)
         for p in range(4):
-            at = pl.ds(rows.start + 32 * p, 32)
+            at = pl.ds(part.start + 32 * p, 32)
             basis[m, at, :] = (second[m, at, :] - coef * probe[m, at, :]) * scale
         stores.append(
-            pltpu.make_async_copy(basis.at[m, rows], basis_hbm.at[m, rows], sems.at[12 + i])
+            pltpu.make_async_copy(basis.at[m, part], basis_hbm.at[m, part], sems.at[i])
         )
         stores[-1].start()
     for store in stores:
@@ -649,7 +637,7 @@
 
 def shards(slabs, columns, state, direction, xxt_rows, coarse_ids):
     shape = state.shape
-    left, right = constants()
+    ops = constants()
     vmem = pltpu.VMEM
     field = (3, 256, 256)
     halved = (3, 2, 256, 128)
@@ -665,15 +653,14 @@
             jax.ShapeDtypeStruct(field, F32),
             jax.ShapeDtypeStruct((8, 128), F32),
         ),
-        in_specs=[pl.BlockSpec(memory_space=pltpu.HBM)] * 6,
+        in_specs=[pl.BlockSpec(memory_space=pltpu.HBM)] * 5,
         out_specs=(anywhere, anywhere, pl.BlockSpec(memory_space=vmem)),
         scratch_shapes=[
             vmem(field, F32),
             vmem(field, F32),
             vmem((32, 8192), F32),
             vmem((1, 128), jnp.int32),
-            vmem((768, 512), BF16),
-            vmem((256, 256), BF16),
+            vmem((896, 512), BF16),
             vmem((2, 32, 256), F32),
             vmem((2,) + field, BF16),
             vmem((2,) + field, BF16),
@@ -704,7 +691,7 @@
             vmem((2, 4, 4, 256), F32),
             vmem((1, 128), F32),
             vmem((256, 128), F32),
-            pltpu.SemaphoreType.DMA((11,)),
+            pltpu.SemaphoreType.DMA((10,)),
             pltpu.SemaphoreType.DMA((4,)),
             pltpu.SemaphoreType.DMA((2, 8)),
             pltpu.SemaphoreType.DMA((2, 8)),
@@ -720,25 +707,21 @@
         direction.reshape(field),
         xxt_rows,
         coarse_ids,
-        jnp.asarray(left),
-        jnp.asarray(right),
+        jnp.asarray(ops),
     )
     next_basis, hessenberg = pl.pallas_call(
         normalise,
         out_shape=(jax.ShapeDtypeStruct(field, F32), jax.ShapeDtypeStruct((2,), F32)),
-        in_specs=[pl.BlockSpec(memory_space=pltpu.HBM)] * 3,
+        in_specs=[pl.BlockSpec(memory_space=vmem)] * 3,
         out_specs=(
             pl.BlockSpec(memory_space=pltpu.HBM),
             pl.BlockSpec(memory_space=pltpu.SMEM),
         ),
         scratch_shapes=[
             vmem(field, F32),
-            vmem(field, F32),
-            vmem((8, 128), F32),
-            vmem(field, F32),
-            pltpu.SemaphoreType.DMA((19,)),
+            pltpu.SemaphoreType.DMA((6,)),
         ],
-        compiler_params=pltpu.CompilerParams(vmem_limit_bytes=VMEM_LIMIT),
+        compiler_params=pltpu.CompilerParams(vmem_limit_bytes=16 * 1024 * 1024),
         name="normalise",
     )(sec, probe, scal)
     return next_basis.reshape(shape), hessenberg

time: 50.5 us -> 49 us (0.970)
  Pallas kernels: 49.7 us -> 47.6 us
  local copies, waits for them, and re-layouts: 0 us -> 0.65 us
    pallas_call x1, Pallas kernels: 2.8 us -> 1.49 us  [shards(): pl.pallas_call(normalise, out_shape=(jax.ShapeDtypeStruct(field, F32), ja...]
    pallas_call x1, Pallas kernels: 46.9 us -> 46.1 us  [shards(): pl.pallas_call(body, out_shape=(jax.ShapeDtypeStruct(field, F32), jax.Sha...]
    unnamed x0 -> x2, local copies, waits for them, and re-layouts: none -> 0.65 us
where the time goes in v4:
time: 49 us; the launch traced here: 48.9 us
  Pallas kernels  47.6 us (97%)
  local copies, waits for them, and re-layouts  0.65 us (1%)
  between operations  0.65 us (1%)
    pallas_call x1, Pallas kernels, shards(): pl.pallas_call(body, out_shape=(jax.ShapeDtypeStruct(field, F32), jax.Sha...  46.1 us
    pallas_call x1, Pallas kernels, shards(): pl.pallas_call(normalise, out_shape=(jax.ShapeDtypeStruct(field, F32), ja...  1.49 us

profile of v4, /device:TPU:1, one launch (start us, length us, event | category | flops | bytes accessed | tf_op | source)
XLA Modules:
  0.0 48.9 jit_solution(3301364872849936930)
XLA Ops:
  0.6 0.0 copy-start
  0.6 0.6 %copy-done = s32[1,128]{1,0:T(1,128)S(1)} copy-done((s32[1,128]{1,0:T(1,128)S(1)}, s32[1,128]{1,0:T(1,128)}, u32[]{:S(2)}) %copy-start) | copy-done | bytes 536
  1.3 46.1 %jacobian_products.1 = (f32[3,256,256]{2,1,0:T(8,128)S(1)}, f32[3,256,256]{2,1,0:T(8,128)S(1)}, f32[8,128]{1,0:T(8,128)S(1)}) custom-call(f32[3,256,256]{2,1,0:T(8,128)} %bitcast.3, f32[3,256,256]{2,1,0:T(8,128)} %bitcast.4, f32[32,8192]{1,0:T(8,128)} %refs_2_.1, s32[1,128]{1,0:T(1,128)S(1)} %copy-done, bf16[896,512]{1,0:T(8,128)(2,1)} %constant.2.clone.refs_4_), custom_call_target="tpu_custom_call" | custom-call | tf_op jit(solution)/shard_map/jacobian_products/pallas_call | solution.py:649
  47.4 1.5 %normalise.1 = (f32[3,256,256]{2,1,0:T(8,128)}, f32[2]{0:T(128)}) custom-call(f32[3,256,256]{2,1,0:T(8,128)S(1)} %get-tuple-element.7.second, f32[3,256,256]{2,1,0:T(8,128)S(1)} %get-tuple-element.8.probe, f32[8,128]{1,0:T(8,128)S(1)} %get-tuple-element.9.scal), custom_call_target="tpu_custom_call" | custom-call | tf_op jit(solution)/shard_map/normalise/pallas_call | solution.py:712
Async XLA Ops:
  0.6 0.7 %copy-start = (s32[1,128]{1,0:T(1,128)S(1)}, s32[1,128]{1,0:T(1,128)}, u32[]{:S(2)}) copy-start(s32[1,128]{1,0:T(1,128)} %refs_3_.1) | copy-start | bytes 1540

commit v5 on v4

--- a/solution.py
+++ b/solution.py
@@ -52,7 +52,8 @@
     return derivative, weights
 
 
-GROUPS = ((0, 64, (0, 7)), (192, 192, (1, 2, 3, 4, 5, 6)))
+X_ORDER = (0, 7, 1, 2, 3, 4, 5, 6)
+GROUPS = ((0, 2, (0, 7)), (2, 8, (1, 2, 3, 4, 5, 6)))
 DIMS = {"z": 8, "x": 4, "y": 4, "c": 2}
 
 
@@ -78,26 +79,20 @@
 def constants():
     derivative, weights = tables()
     stiff = viscosity * (derivative.T * weights[None, :]) @ derivative / weights[:, None]
-    eye = np.eye
-    along_x = np.kron(derivative, eye(32))
-    along_y = np.kron(eye(32), derivative)
-    spread_xy = np.kron(stiff, eye(32)) + np.kron(eye(32), stiff)
-    left = [
-        op[32 * plane : 32 * plane + 32]
-        for _, _, planes in GROUPS
-        for op in (along_x, along_y, spread_xy)
-        for plane in planes
+    eye, order = np.eye, np.array(X_ORDER)
+    derivative_x, stiff_x = (op[order][:, order] for op in (derivative, stiff))
+    ops = [
+        np.kron(derivative_x, eye(8)),
+        np.kron(eye(8), derivative),
+        np.kron(stiff_x, eye(8)) + np.kron(eye(8), stiff),
     ]
-    left = np.concatenate(left, axis=0)
+    left = [op[8 * start : 8 * end] for start, end, _ in GROUPS for op in ops]
+    high, low = halves(np.concatenate(left, axis=0))
     right = np.concatenate([np.kron(eye(16), derivative.T), np.kron(eye(16), stiff.T)], axis=1)
-    return np.concatenate(
-        [
-            np.concatenate(halves(left[:192]), axis=1),
-            np.concatenate(halves(right), axis=1),
-            np.concatenate(halves(left[192:]), axis=1),
-        ],
-        axis=0,
-    )
+    table = np.zeros((1024, 512), ml_dtypes.bfloat16)
+    table[:192, :256] = np.concatenate([high, low, high, low], axis=1)
+    table[192:320] = np.concatenate(halves(right), axis=1)
+    return table
 
 
 WEIGHTS = tables()[1]
@@ -123,7 +118,8 @@
     direc,
     xxt,
     ids,
-    ops_all,
+    left,
+    right,
     plane,
     highs,
     lows,
@@ -165,30 +161,31 @@
     gz, px = gx // 4, gx % 4
     here = px * columns + yz
 
+    z_at = [jnp.bitwise_and(gz + k, 7) * 4 for k in range(8)]
+    x_at = [jnp.bitwise_and(px + k, 3) for k in range(4)]
+    y_at = [jnp.bitwise_and(yz // 2 + k, 3) * 2 for k in range(4)]
+    c_at = [jnp.bitwise_and(yz + k, 1) for k in range(2)]
+
     def peer_at(place):
-        z = lax.rem(gz + place.get("z", 0), 8)
-        x = lax.rem(px + place.get("x", 0), 4)
-        y = lax.rem(yz // 2 + place.get("y", 0), 4)
-        c = lax.rem(yz % 2 + place.get("c", 0), 2)
-        return (z * 4 + x, y * 2 + c)
+        z, x, y, c = (place.get(name, 0) for name in "zxyc")
+        return (z_at[z] + x_at[x], y_at[y] + c_at[c])
 
     in_plane, in_ring, everyone = offsets("xyc"), offsets("z"), offsets("zxyc")
 
     def beside(dx, dy):
         return (lax.rem(gx + dx + slabs, slabs), lax.rem(yz + dy + columns, columns))
 
-    first, others = pl.ds(0, 320), pl.ds(320, 576)
-    pairs = [(ops_hbm.at[first], ops_all.at[first])]
+    pairs = [(ops_hbm.at[pl.ds(0, 192), pl.ds(0, 256)], left)]
+    pairs += [(ops_hbm.at[pl.ds(192, 128)], right)]
     pairs += [(state_hbm.at[m], state.at[m]) for m in range(3)]
     pairs += [(dir_hbm.at[m], direc.at[m]) for m in range(3)]
-    pairs += [(ops_hbm.at[others], ops_all.at[others])]
     pairs += [(ids_hbm, ids), (xxt_hbm, xxt)]
     loads = [pltpu.make_async_copy(src, dst, in_sem.at[i]) for i, (src, dst) in enumerate(pairs)]
     for load in loads[:-1]:
         load.start()
 
     barrier = pltpu.get_barrier_semaphore()
-    greeted = [peer_at(place) for _, place in in_plane + in_ring]
+    greeted = [peer_at(place) for _, place in in_ring + in_plane]
     greeted += [beside(dx, dy) for dx in (-1, 1) for dy in (-1, 0, 1)]
     for peer in greeted:
         pl.semaphore_signal(barrier, inc=1, device_id=peer, device_id_type=MESH)
@@ -238,30 +235,35 @@
     def whole(ref, m, rows):
         return ref[m, rows, :]
 
-    def split_into(value, which, m):
-        high, low = split(value)
-        highs[which, m] = high
-        lows[which, m] = low
-
-    def products_left(which, m, g, count):
-        first, rows, _ = GROUPS[g]
-        ops = ops_all[pl.ds(first + 128 * g, rows * count), :]
-        high, low = highs[which, m], lows[which, m]
+    def places_of(g, b):
+        start, end, _ = GROUPS[g]
+        return [(8 * (i - start), pl.ds(32 * X_ORDER[i] + 8 * b, 8)) for i in range(start, end)]
+
+    def split_into(take, vector, which, m):
+        for b in range(4):
+            pieces = [take(vector, m, pl.ds(32 * x + 8 * b, 8)) for x in X_ORDER]
+            high, low = split(jnp.concatenate(pieces, axis=0))
+            highs[which, m, b] = high
+            lows[which, m, b] = low
+
+    def products_left(which, m, b, g, count):
+        start, size = ((0, 16), (48, 48))[g]
+        high, low = highs[which, m, b], lows[which, m, b]
         return jnp.dot(
-            jnp.concatenate([ops, ops[:, :256]], axis=1),
-            jnp.concatenate([high, high, low], axis=0),
+            left[pl.ds(start, size * count), :],
+            jnp.concatenate([high, high, low, low], axis=0),
             preferred_element_type=F32,
         )
 
     def products_right(which, m, g, cols):
-        at = pl.ds(192, 128)
-        high, low = (ops_all[at, pl.ds(start, cols)] for start in (0, 256))
+        high, low = (right[:, pl.ds(start, cols)] for start in (0, 256))
         ops = jnp.concatenate([high, low, high], axis=0)
+        rows = (pl.ds(0, 16), pl.ds(16, 48))[g]
         results = []
         for h in range(2):
             high, low = (
                 jnp.concatenate(
-                    [ref[which, m, rows_of(p), pl.ds(128 * h, 128)] for p in GROUPS[g][2]], axis=0
+                    [ref[which, m, b, rows, pl.ds(128 * h, 128)] for b in range(4)], axis=0
                 )
                 for ref in (highs, lows)
             )
@@ -270,40 +272,45 @@
         return results
 
     def state_gradients(m, g):
-        _, size, planes = GROUPS[g]
-        by_left = products_left(0, m, g, 2)
-        by_right = jnp.concatenate(products_right(0, m, g, 128), axis=1)
-        for i, p in enumerate(planes):
-            grads[m, 0, rows_of(p), :] = by_left[32 * i : 32 * i + 32]
-            grads[m, 1, rows_of(p), :] = by_left[size + 32 * i : size + 32 * i + 32]
-            grads[m, 2, rows_of(p), :] = by_right[32 * i : 32 * i + 32]
+        size = (16, 48)[g]
+        one, two = products_right(0, m, g, 128)
+        for b in range(4):
+            by_left = products_left(0, m, b, g, 2)
+            for at, rows in places_of(g, b):
+                for op in range(2):
+                    grads[m, op, rows, :] = by_left[size * op + at : size * op + at + 8]
+                at += size * b
+                grads[m, 2, rows, :] = jnp.concatenate([one[at : at + 8], two[at : at + 8]], axis=1)
 
     def multiply(which, m, g):
-        first, size, planes = GROUPS[g]
-        lhs_out[m, pl.ds(first, 3 * size), :] = products_left(which, m, g, 3)
-        for h, by_right in enumerate(products_right(which, m, g, 256)):
-            for i, p in enumerate(planes):
-                rhs_out[m, h, rows_of(p), :] = by_right[32 * i : 32 * i + 32]
+        size = (16, 48)[g]
+        by_right = products_right(which, m, g, 256)
+        for b in range(4):
+            by_left = products_left(which, m, b, g, 3)
+            for at, rows in places_of(g, b):
+                for op in range(3):
+                    lhs_out[m, op, rows, :] = by_left[size * op + at : size * op + at + 8]
+                at += size * b
+                for h in range(2):
+                    rhs_out[m, h, rows, :] = by_right[h][at : at + 8]
 
     def along_z(m, rows, kind):
         part = pl.ds(128 * kind, 128)
         return jnp.concatenate([rhs_out[m, 0, rows, part], rhs_out[m, 1, rows, part]], axis=1)
 
     def combine(vector, take, m, g, target):
-        first, size, planes = GROUPS[g]
-        for i, p in enumerate(planes):
+        for p in GROUPS[g][2]:
             rows = rows_of(p)
-            at = [pl.ds(first + size * op + 32 * i, 32) for op in range(3)]
-            total = lhs_out[m, at[2], :] + along_z(m, rows, 1)
-            total += state[0, rows, :] * lhs_out[m, at[0], :]
-            total += state[1, rows, :] * lhs_out[m, at[1], :]
+            total = lhs_out[m, 2, rows, :] + along_z(m, rows, 1)
+            total += state[0, rows, :] * lhs_out[m, 0, rows, :]
+            total += state[1, rows, :] * lhs_out[m, 1, rows, :]
             total += state[2, rows, :] * along_z(m, rows, 0)
             for k in range(3):
                 total += take(vector, k, rows) * grads[m, k, rows, :]
             put(target, m, rows, total * (plane[0] * float(WEIGHTS[p])))
 
     def apply_to_image(m):
-        split_into(get(image, m, pl.ds(0, 256)), 1, m)
+        split_into(get, image, 1, m)
         for g in range(2):
             multiply(1, m, g)
             combine(image, get, m, g, local2)
@@ -390,13 +397,14 @@
         pltpu.make_async_copy(ref, ref, sem).wait()
 
     loads[0].wait()
-    for m in range(3):
-        loads[1 + m].wait()
-        split_into(state[m], 0, m)
+    loads[1].wait()
+    for m in range(3):
+        loads[2 + m].wait()
+        split_into(whole, state, 0, m)
         state_gradients(m, 0)
     for m in range(3):
-        loads[4 + m].wait()
-        split_into(direc[m], 1, m)
+        loads[5 + m].wait()
+        split_into(whole, direc, 1, m)
     for m in range(3):
         multiply(1, m, 0)
         combine(direc, whole, m, 0, local)
@@ -405,7 +413,6 @@
         send_x(0, local, m)
     send_corners(0, local)
     loads[9].start()
-    loads[7].wait()
     for m in range(3):
         state_gradients(m, 1)
         multiply(1, m, 1)
@@ -660,12 +667,13 @@
             vmem(field, F32),
             vmem((32, 8192), F32),
             vmem((1, 128), jnp.int32),
-            vmem((896, 512), BF16),
+            vmem((192, 256), BF16),
+            vmem((128, 512), BF16),
             vmem((2, 32, 256), F32),
-            vmem((2,) + field, BF16),
-            vmem((2,) + field, BF16),
+            vmem((2, 3, 4, 64, 256), BF16),
+            vmem((2, 3, 4, 64, 256), BF16),
             vmem((3, 3, 256, 256), F32),
-            vmem((3, 768, 256), F32),
+            vmem((3, 3, 256, 256), F32),
             vmem((3, 2, 256, 256), F32),
             vmem(halved, F32),
             vmem(halved, F32),

time: 49 us -> 49.1 us (level)
  no operation moved by 1% of the time
where the time goes in v5:
time: 49.1 us; the launch traced here: 49 us
  Pallas kernels  47.7 us (97%)
  local copies, waits for them, and re-layouts  0.65 us (1%)
  between operations  0.65 us (1%)
    pallas_call x1, Pallas kernels, shards(): pl.pallas_call(body, out_shape=(jax.ShapeDtypeStruct(field, F32), jax.Sha...  46.2 us
    pallas_call x1, Pallas kernels, shards(): pl.pallas_call(normalise, out_shape=(jax.ShapeDtypeStruct(field, F32), ja...  1.49 us

profile of v5, /device:TPU:1, one launch (start us, length us, event | category | flops | bytes accessed | tf_op | source)
XLA Modules:
  0.0 49.0 jit_solution(7361740480894835359)
XLA Ops:
  0.6 0.0 copy-start
  0.6 0.6 %copy-done = s32[1,128]{1,0:T(1,128)S(1)} copy-done((s32[1,128]{1,0:T(1,128)S(1)}, s32[1,128]{1,0:T(1,128)}, u32[]{:S(2)}) %copy-start) | copy-done | bytes 536
  1.3 46.2 %jacobian_products.1 = (f32[3,256,256]{2,1,0:T(8,128)S(1)}, f32[3,256,256]{2,1,0:T(8,128)S(1)}, f32[8,128]{1,0:T(8,128)S(1)}) custom-call(f32[3,256,256]{2,1,0:T(8,128)} %bitcast.3, f32[3,256,256]{2,1,0:T(8,128)} %bitcast.4, f32[32,8192]{1,0:T(8,128)} %refs_2_.1, s32[1,128]{1,0:T(1,128)S(1)} %copy-done, bf16[1024,512]{1,0:T(8,128)(2,1)} %constant.2.clone.refs_4_), custom_call_target="tpu_custom_call" | custom-call | tf_op jit(solution)/shard_map/jacobian_products/pallas_call | solution.py:656
  47.5 1.5 %normalise.1 = (f32[3,256,256]{2,1,0:T(8,128)}, f32[2]{0:T(128)}) custom-call(f32[3,256,256]{2,1,0:T(8,128)S(1)} %get-tuple-element.7.second, f32[3,256,256]{2,1,0:T(8,128)S(1)} %get-tuple-element.8.probe, f32[8,128]{1,0:T(8,128)S(1)} %get-tuple-element.9.scal), custom_call_target="tpu_custom_call" | custom-call | tf_op jit(solution)/shard_map/normalise/pallas_call | solution.py:720
Async XLA Ops:
  0.6 0.7 %copy-start = (s32[1,128]{1,0:T(1,128)S(1)}, s32[1,128]{1,0:T(1,128)}, u32[]{:S(2)}) copy-start(s32[1,128]{1,0:T(1,128)} %refs_3_.1) | copy-start | bytes 1540

commit v6 on v5

--- a/solution.py
+++ b/solution.py
@@ -175,6 +175,12 @@
     def beside(dx, dy):
         return (lax.rem(gx + dx + slabs, slabs), lax.rem(yz + dy + columns, columns))
 
+    barrier = pltpu.get_barrier_semaphore()
+    greeted = [peer_at(place) for _, place in in_plane + in_ring]
+    greeted += [beside(dx, dy) for dx in (-1, 1) for dy in (-1, 0, 1)]
+    for peer in greeted:
+        pl.semaphore_signal(barrier, inc=1, device_id=peer, device_id_type=MESH)
+
     pairs = [(ops_hbm.at[pl.ds(0, 192), pl.ds(0, 256)], left)]
     pairs += [(ops_hbm.at[pl.ds(192, 128)], right)]
     pairs += [(state_hbm.at[m], state.at[m]) for m in range(3)]
@@ -183,12 +189,6 @@
     loads = [pltpu.make_async_copy(src, dst, in_sem.at[i]) for i, (src, dst) in enumerate(pairs)]
     for load in loads[:-1]:
         load.start()
-
-    barrier = pltpu.get_barrier_semaphore()
-    greeted = [peer_at(place) for _, place in in_ring + in_plane]
-    greeted += [beside(dx, dy) for dx in (-1, 1) for dy in (-1, 0, 1)]
-    for peer in greeted:
-        pl.semaphore_signal(barrier, inc=1, device_id=peer, device_id_type=MESH)
 
     lane = lax.broadcasted_iota(jnp.int32, (1, 256), 1)
     from_next = ((lane % 8 == 7) & (lane != 255)).astype(F32)

time: 49.1 us -> 49 us (level)
  no operation moved by 1% of the time
where the time goes in v6:
time: 49 us; the launch traced here: 48.9 us
  Pallas kernels  47.6 us (97%)
  local copies, waits for them, and re-layouts  0.65 us (1%)
  between operations  0.65 us (1%)
    pallas_call x1, Pallas kernels, shards(): pl.pallas_call(body, out_shape=(jax.ShapeDtypeStruct(field, F32), jax.Sha...  46.1 us
    pallas_call x1, Pallas kernels, shards(): pl.pallas_call(normalise, out_shape=(jax.ShapeDtypeStruct(field, F32), ja...  1.49 us

profile of v6, /device:TPU:1, one launch (start us, length us, event | category | flops | bytes accessed | tf_op | source)
XLA Modules:
  0.0 48.9 jit_solution(5980624551851253144)
XLA Ops:
  0.6 0.0 copy-start
  0.6 0.6 %copy-done = s32[1,128]{1,0:T(1,128)S(1)} copy-done((s32[1,128]{1,0:T(1,128)S(1)}, s32[1,128]{1,0:T(1,128)}, u32[]{:S(2)}) %copy-start) | copy-done | bytes 536
  1.3 46.1 %jacobian_products.1 = (f32[3,256,256]{2,1,0:T(8,128)S(1)}, f32[3,256,256]{2,1,0:T(8,128)S(1)}, f32[8,128]{1,0:T(8,128)S(1)}) custom-call(f32[3,256,256]{2,1,0:T(8,128)} %bitcast.3, f32[3,256,256]{2,1,0:T(8,128)} %bitcast.4, f32[32,8192]{1,0:T(8,128)} %refs_2_.1, s32[1,128]{1,0:T(1,128)S(1)} %copy-done, bf16[1024,512]{1,0:T(8,128)(2,1)} %constant.2.clone.refs_4_), custom_call_target="tpu_custom_call" | custom-call | tf_op jit(solution)/shard_map/jacobian_products/pallas_call | solution.py:656
  47.4 1.5 %normalise.1 = (f32[3,256,256]{2,1,0:T(8,128)}, f32[2]{0:T(128)}) custom-call(f32[3,256,256]{2,1,0:T(8,128)S(1)} %get-tuple-element.7.second, f32[3,256,256]{2,1,0:T(8,128)S(1)} %get-tuple-element.8.probe, f32[8,128]{1,0:T(8,128)S(1)} %get-tuple-element.9.scal), custom_call_target="tpu_custom_call" | custom-call | tf_op jit(solution)/shard_map/normalise/pallas_call | solution.py:720
Async XLA Ops:
  0.6 0.7 %copy-start = (s32[1,128]{1,0:T(1,128)S(1)}, s32[1,128]{1,0:T(1,128)}, u32[]{:S(2)}) copy-start(s32[1,128]{1,0:T(1,128)} %refs_3_.1) | copy-start | bytes 1540
